TPU v7x, 128 devices: a whole 4x4x4 slice. The times are simulated.
128 devices in a mesh: grp: 8 (over y, core), row: 16 (over z, x).
Axes of the slice: x: 4, y: 4, z: 4, core: 2. Of those that a mesh axis runs over, the one named last changes fastest.
Arguments:
- a_blocks: bfloat16 [327680, 512], P(('grp', 'row')), may hold values from -0.25 to 0.25
- a_cols: int32 [5120, 8], P(('grp', 'row')), may hold values from 0 to 5119, as said below
- a_count: int32 [5120], P(('grp', 'row')), may hold values from 2 to 8, as said below
- p_blocks: bfloat16 [327680, 256], P(('grp', 'row')), may hold values from -0.75 to 0.75
- p_cols: int32 [5120, 4], P(('grp', 'row')), may hold values from 0 to 1279, as said below
- q2_blocks: bfloat16 [1280, 4096], P(('grp', 'row')), may hold values from -0.75 to 0.75
- agg3: int32 [1280], P(('grp', 'row')), may hold values from 0 to 95, as said below
Outputs:
- level2_op: bfloat16 [81920, 3200], P(('grp', 'row'))
- level3_op: float32 [6144, 2304], P('grp')
Inputs may be any that keep to these rules, and one draw needn't show every extreme that they name: a_cols[i, 0] = i, and every a_cols[i, k] differs from i by at most 40. `a_count`: block rows i with i % 40 == 0 use all 8 blocks. `p_cols`: the 4 entries of a row are distinct and lie from 10 (i // 40) to 10 (i // 40 + 2) - 1 for block row i. agg3[c] lies from 12 g to 12 (g + 1) - 1 with g = c // 160.
All inputs are finite; a program needn't handle non-finite values.
Results may differ from a plain program's by a relative error of at most 0.0058.
Values may be sent and summed in bfloat16 or wider, within the bound.
No kernel may reach another device: no remote copies, remote signals or barrier semaphores. Data moves between devices by JAX's collectives and lax.ppermute only.
A program may use at most 128 MiB of HBM per device.

v0:
```python
import jax
import jax.numpy as jnp
from jax import lax
from jax.sharding import PartitionSpec as P

B = 64
KA = 8
KP = 4
A3G = 12


def padded(array, sides, width):
    for axis, dim in sides:
        devices, length = (lax.axis_size(axis), array.shape[dim])
        up = [(i, (i + 1) % devices) for i in range(devices - 1)]
        down = [(j, i) for i, j in up]
        last = lax.slice_in_dim(array, length - width, length, axis=dim)
        leading = lax.slice_in_dim(array, 0, width, axis=dim)
        before = lax.ppermute(last, axis, up)
        after = lax.ppermute(leading, axis, down)
        array = jnp.concatenate([before, array, after], axis=dim)
    return array


def passed_along(array, axis, by):
    devices = lax.axis_size(axis)
    pairs = [(i, i + by) for i in range(devices) if 0 <= i + by < devices]
    return lax.ppermute(array, axis, pairs)


def per_device(a_blocks, a_cols, a_count, p_blocks, p_cols, q2_blocks, agg3):
    highest_precision_flag = lax.Precision.HIGHEST
    rows_dev = a_cols.shape[0]
    coarse_dev = q2_blocks.shape[0]
    band = coarse_dev * B
    device = lax.axis_index(("grp", "row"))
    row_size = lax.axis_size("row")
    group = device // row_size
    ext_p = padded(p_blocks, ((("grp", "row"), 0),), rows_dev * B)
    ext_cols = padded(p_cols, ((("grp", "row"), 0),), rows_dev)
    ext_p = ext_p.reshape(3 * rows_dev, B, KP * B)
    turns = rows_dev // 4
    blk_a = a_blocks.reshape(turns, 4, B, KA, B)
    blk_cols = a_cols.reshape(turns, 4, KA)
    blk_count = a_count.reshape(turns, 4)
    blk_p = p_blocks.reshape(turns, 4, B, KP, B)
    blk_pc = p_cols.reshape(turns, 4, KP)
    wide_ids = jnp.arange(4 * coarse_dev, dtype=jnp.int32)
    own_ids = jnp.arange(2 * coarse_dev, dtype=jnp.int32)
    slots = jnp.arange(KA, dtype=jnp.int32)

    def accumulate_block_entry(total, pieces):
        amat, cols, count, pmat, pcols = pieces
        keep = slots[None, :] < count[:, None]
        amat = jnp.where(keep[:, None, :, None], amat, jnp.zeros_like(amat))
        local = cols - (device - 1) * rows_dev
        prow = ext_p[local]
        pattern = ext_cols[local] - (device - 1) * coarse_dev
        hot = (pattern[..., None] == wide_ids).astype(jnp.float32)
        prod = jnp.einsum("rfkg,rkgq->rkfq", amat, prow, preferred_element_type=jnp.float32)
        prod = prod.reshape(prod.shape[0], KA, B, KP, B)
        wide = jnp.einsum("rkfmq,rkmc->rfcq", prod, hot, precision=highest_precision_flag).astype(
            jnp.bfloat16
        )
        wide = wide.reshape(wide.shape[0], B, 4 * band)
        part = jnp.einsum("rfmq,rfx->rmqx", pmat, wide, preferred_element_type=jnp.float32)
        owner_hot = ((pcols - device * coarse_dev)[..., None] == own_ids).astype(jnp.float32)
        return (
            total + jnp.einsum("rmt,rmqx->tqx", owner_hot, part, precision=highest_precision_flag),
            None,
        )

    start = jnp.zeros((2 * coarse_dev, B, 4 * band), jnp.float32)
    total, unused = lax.scan(
        accumulate_block_entry, start, (blk_a, blk_cols, blk_count, blk_p, blk_pc)
    )
    total = total.reshape(2 * band, 4 * band)
    sent = passed_along(total[band:], ("grp", "row"), 1)
    level2 = jnp.pad(total[:band], ((0, 0), (band, 0))) + jnp.pad(sent, ((0, 0), (0, band)))
    coarse = level2.astype(jnp.bfloat16)
    near_q = padded(q2_blocks, ((("grp", "row"), 0),), coarse_dev)
    near_agg = padded(agg3, ((("grp", "row"), 0),), coarse_dev)
    lower_q = passed_along(q2_blocks, ("grp", "row"), 2)
    lower_agg = passed_along(agg3, ("grp", "row"), 2)
    upper_q = passed_along(q2_blocks, ("grp", "row"), -2)
    upper_agg = passed_along(agg3, ("grp", "row"), -2)
    ext_q = jnp.concatenate([lower_q, near_q, upper_q], axis=0)
    ext_agg = jnp.concatenate([lower_agg, near_agg, upper_agg], axis=0)
    ext_q = ext_q.reshape(5 * coarse_dev, B, B)
    slot_ids = jnp.arange(3 * A3G, dtype=jnp.int32)
    block_position = ((ext_agg - (group - 1) * A3G)[:, None] == slot_ids).astype(jnp.float32)
    coarse_three = coarse.reshape(band, 5 * coarse_dev, B)
    galerkin_triple_products = jnp.einsum(
        "rjp,jpq->rjq", coarse_three, ext_q, preferred_element_type=jnp.float32
    )
    mixed_precision_result = jnp.einsum(
        "ead,ao->eod", galerkin_triple_products, block_position, precision=highest_precision_flag
    ).astype(jnp.bfloat16)
    mixed_precision_result = mixed_precision_result.reshape(coarse_dev, B, 3 * A3G * B)
    blocks_q = q2_blocks.reshape(coarse_dev, B, B)
    terms = jnp.einsum(
        "cpq,cpx->cqx", blocks_q, mixed_precision_result, preferred_element_type=jnp.float32
    )
    own_hot = ((agg3 - group * A3G)[:, None] == jnp.arange(A3G, dtype=jnp.int32)).astype(
        jnp.float32
    )
    share_sum = jnp.einsum("ca,cqx->aqx", own_hot, terms, precision=highest_precision_flag).reshape(
        A3G * B, 3 * A3G * B
    )
    level3 = lax.psum(share_sum, "row")
    return (coarse, level3)


def solution(mesh):
    in_specs = (
        P(("grp", "row"), None),
        P(("grp", "row"), None),
        P(("grp", "row")),
        P(("grp", "row"), None),
        P(("grp", "row"), None),
        P(("grp", "row"), None),
        P(("grp", "row")),
    )
    out_specs = (P(("grp", "row"), None), P("grp", None))
    return jax.shard_map(
        per_device, mesh=mesh, in_specs=in_specs, out_specs=out_specs, check_vma=False
    )
```

profile of v0, /device:TPU:8, one launch (start us, length us, event | category | flops | bytes accessed | tf_op | source)
XLA Modules:
  0.0 1037.6 jit_solution(8862471941585860744)
XLA Ops:
  7.2 7.6 collective-permute-start.3
  16.8 7.9 collective-permute-start.1
  33.7 7.5 reshape.161
  44.2 8.2 collective-permute-done
  55.7 561.9 %while.13 = (s32[]{:T(128)}, f32[20,64,2560]{2,0,1:T(8,128)}, s32[10,4,4]{2,1,0:T(4,128)S(1)}, s32[]{:T(128)}, bf16[10,4,64,4,64]{4,3,2,1,0:T(4,128)(2,1)}, /*in...) while((s32[]{:T(128)}, f32[20,64,2560]{2,0,1:T(8,128)}, ...), condition=%wide.region_1.2_spmd.clone, body=%wide.region_0.1_spmd.clone.sunk | while | flops 1290803712 | bytes 65414116 | solution.py:74
  64.2 7.4 fusion.74
  82.2 27.7 %bitcast_add_fusion.2 = f32[20,64,2560]{2,0,1:T(8,128)} fusion(f32[20,64,2560]{2,0,1:T(8,128)} %get-tuple-element.385, pred[]{:T(512)S(6)} %compare.7, f32[4,4,64,2560]{3,2,1,0:T(8,128)} %fusion.75, s32[4,4]{0,1:T(4,128)S(1)} %copy.153), kind=kOutput, calls=%fused_computation.5.clone.1 | convolution fusion | flops 635699520 | bytes 36700224 | tf_op jit(solution)/shard_map/while/body/eval_jaxpr/rmt,rmqx->tqx/dot_general | solution.py:69
  118.2 7.4 fusion.74
  136.3 30.0 %bitcast_add_fusion.2 = f32[20,64,2560]{2,0,1:T(8,128)} fusion(f32[20,64,2560]{2,0,1:T(8,128)} %get-tuple-element.385, pred[]{:T(512)S(6)} %compare.7, f32[4,4,64,2560]{3,2,1,0:T(8,128)} %fusion.75, s32[4,4]{0,1:T(4,128)S(1)} %copy.153), kind=kOutput, calls=%fused_computation.5.clone.1 | convolution fusion | flops 635699520 | bytes 36700224 | tf_op jit(solution)/shard_map/while/body/eval_jaxpr/rmt,rmqx->tqx/dot_general | solution.py:69
  174.6 7.4 fusion.74
  192.6 30.0 %bitcast_add_fusion.2 = f32[20,64,2560]{2,0,1:T(8,128)} fusion(f32[20,64,2560]{2,0,1:T(8,128)} %get-tuple-element.385, pred[]{:T(512)S(6)} %compare.7, f32[4,4,64,2560]{3,2,1,0:T(8,128)} %fusion.75, s32[4,4]{0,1:T(4,128)S(1)} %copy.153), kind=kOutput, calls=%fused_computation.5.clone.1 | convolution fusion | flops 635699520 | bytes 36700224 | tf_op jit(solution)/shard_map/while/body/eval_jaxpr/rmt,rmqx->tqx/dot_general | solution.py:69
  230.9 7.4 fusion.74
  249.0 30.0 %bitcast_add_fusion.2 = f32[20,64,2560]{2,0,1:T(8,128)} fusion(f32[20,64,2560]{2,0,1:T(8,128)} %get-tuple-element.385, pred[]{:T(512)S(6)} %compare.7, f32[4,4,64,2560]{3,2,1,0:T(8,128)} %fusion.75, s32[4,4]{0,1:T(4,128)S(1)} %copy.153), kind=kOutput, calls=%fused_computation.5.clone.1 | convolution fusion | flops 635699520 | bytes 36700224 | tf_op jit(solution)/shard_map/while/body/eval_jaxpr/rmt,rmqx->tqx/dot_general | solution.py:69
  287.3 7.4 fusion.74
  305.4 30.0 %bitcast_add_fusion.2 = f32[20,64,2560]{2,0,1:T(8,128)} fusion(f32[20,64,2560]{2,0,1:T(8,128)} %get-tuple-element.385, pred[]{:T(512)S(6)} %compare.7, f32[4,4,64,2560]{3,2,1,0:T(8,128)} %fusion.75, s32[4,4]{0,1:T(4,128)S(1)} %copy.153), kind=kOutput, calls=%fused_computation.5.clone.1 | convolution fusion | flops 635699520 | bytes 36700224 | tf_op jit(solution)/shard_map/while/body/eval_jaxpr/rmt,rmqx->tqx/dot_general | solution.py:69
  343.7 7.4 fusion.74
  361.7 30.0 %bitcast_add_fusion.2 = f32[20,64,2560]{2,0,1:T(8,128)} fusion(f32[20,64,2560]{2,0,1:T(8,128)} %get-tuple-element.385, pred[]{:T(512)S(6)} %compare.7, f32[4,4,64,2560]{3,2,1,0:T(8,128)} %fusion.75, s32[4,4]{0,1:T(4,128)S(1)} %copy.153), kind=kOutput, calls=%fused_computation.5.clone.1 | convolution fusion | flops 635699520 | bytes 36700224 | tf_op jit(solution)/shard_map/while/body/eval_jaxpr/rmt,rmqx->tqx/dot_general | solution.py:69
  400.0 7.4 fusion.74
  418.1 30.0 %bitcast_add_fusion.2 = f32[20,64,2560]{2,0,1:T(8,128)} fusion(f32[20,64,2560]{2,0,1:T(8,128)} %get-tuple-element.385, pred[]{:T(512)S(6)} %compare.7, f32[4,4,64,2560]{3,2,1,0:T(8,128)} %fusion.75, s32[4,4]{0,1:T(4,128)S(1)} %copy.153), kind=kOutput, calls=%fused_computation.5.clone.1 | convolution fusion | flops 635699520 | bytes 36700224 | tf_op jit(solution)/shard_map/while/body/eval_jaxpr/rmt,rmqx->tqx/dot_general | solution.py:69
  474.5 30.0 %bitcast_add_fusion.2 = f32[20,64,2560]{2,0,1:T(8,128)} fusion(f32[20,64,2560]{2,0,1:T(8,128)} %get-tuple-element.385, pred[]{:T(512)S(6)} %compare.7, f32[4,4,64,2560]{3,2,1,0:T(8,128)} %fusion.75, s32[4,4]{0,1:T(4,128)S(1)} %copy.153), kind=kOutput, calls=%fused_computation.5.clone.1 | convolution fusion | flops 635699520 | bytes 36700224 | tf_op jit(solution)/shard_map/while/body/eval_jaxpr/rmt,rmqx->tqx/dot_general | solution.py:69
  530.8 30.0 %bitcast_add_fusion.2 = f32[20,64,2560]{2,0,1:T(8,128)} fusion(f32[20,64,2560]{2,0,1:T(8,128)} %get-tuple-element.385, pred[]{:T(512)S(6)} %compare.7, f32[4,4,64,2560]{3,2,1,0:T(8,128)} %fusion.75, s32[4,4]{0,1:T(4,128)S(1)} %copy.153), kind=kOutput, calls=%fused_computation.5.clone.1 | convolution fusion | flops 635699520 | bytes 36700224 | tf_op jit(solution)/shard_map/while/body/eval_jaxpr/rmt,rmqx->tqx/dot_general | solution.py:69
  569.1 7.4 fusion.74
  587.2 30.0 %bitcast_add_fusion.2 = f32[20,64,2560]{2,0,1:T(8,128)} fusion(f32[20,64,2560]{2,0,1:T(8,128)} %get-tuple-element.385, pred[]{:T(512)S(6)} %compare.7, f32[4,4,64,2560]{3,2,1,0:T(8,128)} %fusion.75, s32[4,4]{0,1:T(4,128)S(1)} %copy.153), kind=kOutput, calls=%fused_computation.5.clone.1 | convolution fusion | flops 635699520 | bytes 36700224 | tf_op jit(solution)/shard_map/while/body/eval_jaxpr/rmt,rmqx->tqx/dot_general | solution.py:69
  617.6 17.8 %copy.104 = f32[20,64,2560]{2,1,0:T(8,128)} copy(f32[20,64,2560]{2,0,1:T(8,128)} %get-tuple-element.163) | data formatting | bytes 26214400 | tf_op jit(solution)/shard_map/while | solution.py:74
  635.4 11.2 %fusion.43 = (f32[10,64,2560]{2,1,0:T(8,128)}, f32[10,64,2560]{2,1,0:T(8,128)}) fusion(f32[20,64,2560]{2,1,0:T(8,128)} %copy.104), kind=kLoop, calls=%fused_computation.54 | loop fusion | bytes 26214400 | tf_op jit(solution)/shard_map/slice | solution.py:79
  652.3 7.9 collective-permute-start.11
  662.4 133.3 %collective-permute-done.5 = s32[10]{0:T(128)S(1)} collective-permute-done((s32[10]{0:T(128)S(1)}, s32[10]{0:T(128)S(1)}, u32[]{:S(2)}, u32[]{:S(2)}) %collective-permute-start.5) | collective-permute-done | bytes 72 | tf_op jit(solution)/shard_map/ppermute | solution.py:28
  845.1 8.3 convert_bitcast_fusion
  853.4 12.2 %copy.109 = bf16[640,36,64]{2,1,0:T(8,128)(2,1)} copy(bf16[640,36,64]{0,1,2:T(8,128)(2,1)S(1)} %convert_bitcast_fusion) | data formatting | bytes 5898240 | tf_op jit(solution)/shard_map/convert_element_type | solution.py:98
  865.7 8.2 reshape.165
  874.8 8.1 fusion.31
  890.0 134.1 %all-reduce.4.cloned.1.call-done = f32[768,2304]{1,0:T(8,128)} async-done(((f32[768,2304]{1,0:T(8,128)}), f32[768,2304]{1,0:T(8,128)}) %all-reduce.4.cloned.1.call-update) | async-done | bytes 7077904 | tf_op jit(solution)/shard_map/psum | solution.py:110
  (233 shorter events, 292.5 us)
Async XLA Ops:
  7.2 45.4 %copy-start = (bf16[2560,256]{1,0:T(8,128)(2,1)S(1)}, bf16[2560,256]{1,0:T(8,128)(2,1)}, u32[]{:S(2)}) copy-start(bf16[2560,256]{1,0:T(8,128)(2,1)} %param.12) | copy-start | bytes 3932164
  7.2 45.2 %copy-start.2 = (s32[40,4]{0,1:T(4,128)S(1)}, s32[40,4]{0,1:T(4,128)}, u32[]{:S(2)}) copy-start(s32[40,4]{0,1:T(4,128)} %param.13) | copy-start | bytes 1924
  7.2 1016.9 %all-reduce.4.cloned.1.call-start = ((), (), s32[]{:S(2)}) async-start(), calls=%async_computation | async-start | bytes 14155776 | tf_op jit(solution)/shard_map/psum | solution.py:110
  7.2 45.3 %collective-permute-start.3 = (bf16[2560,256]{1,0:T(8,128)(2,1)}, bf16[2560,256]{1,0:T(8,128)(2,1)S(1)}, u32[]{:S(2)}, u32[]{:S(2)}) collective-permute-start(bf16[2560,256]{1,0:T(8,128)(2,1)} %param.12), channel_id=1, source_target_pairs={{1,0},{2,1},{3,2},{4,3},{5,4},{6,5},{7,6},{8,7},{9,8},{10,9},{11,1... | collective-permute-start | bytes 3932168 | tf_op jit(solution)/shard_map/ppermute | solution.py:20
  14.8 37.7 %collective-permute-start.2 = (bf16[2560,256]{1,0:T(8,128)(2,1)}, bf16[2560,256]{1,0:T(8,128)(2,1)}, u32[]{:S(2)}, u32[]{:S(2)}) collective-permute-start(bf16[2560,256]{1,0:T(8,128)(2,1)} %param.12), channel_id=1, source_target_pairs={{0,1},{1,2},{2,3},{3,4},{4,5},{5,6},{6,7},{7,8},{8,9},{9,10},{10,1... | collective-permute-start | bytes 3932168 | tf_op jit(solution)/shard_map/ppermute | solution.py:19
  16.8 27.4 %collective-permute-start.1 = (s32[40,4]{0,1:T(4,128)}, s32[40,4]{0,1:T(4,128)S(1)}, u32[]{:S(2)}, u32[]{:S(2)}) collective-permute-start(s32[40,4]{0,1:T(4,128)} %param.13), channel_id=1, source_target_pairs={{1,0},{2,1},{3,2},{4,3},{5,4},{6,5},{7,6},{8,7},{9,8},{10,9},{11,1... | collective-permute-start | bytes 1928 | tf_op jit(solution)/shard_map/ppermute | solution.py:20
  24.6 27.7 %collective-permute-start = (s32[40,4]{0,1:T(4,128)}, s32[40,4]{0,1:T(4,128)S(1)}, u32[]{:S(2)}, u32[]{:S(2)}) collective-permute-start(s32[40,4]{0,1:T(4,128)} %param.13), channel_id=1, source_target_pairs={{0,1},{1,2},{2,3},{3,4},{4,5},{5,6},{6,7},{7,8},{8,9},{9,10},{10,1... | collective-permute-start | bytes 1928 | tf_op jit(solution)/shard_map/ppermute | solution.py:19
  635.4 13.1 %copy-start.1 = (bf16[10,4096]{1,0:T(8,128)(2,1)S(1)}, bf16[10,4096]{1,0:T(8,128)(2,1)}, u32[]{:S(2)}) copy-start(bf16[10,4096]{1,0:T(8,128)(2,1)} %param.14) | copy-start | bytes 245764
  635.4 24.8 %copy-start.3 = (s32[10]{0:T(128)S(1)}, s32[10]{0:T(128)}, u32[]{:S(2)}) copy-start(s32[10]{0:T(128)} %param.15) | copy-start | bytes 124
  646.5 180.9 %collective-permute-start.4 = (f32[640,2560]{1,0:T(8,128)}, f32[640,2560]{1,0:T(8,128)}, u32[]{:S(2)}, u32[]{:S(2)}) collective-permute-start(f32[640,2560]{1,0:T(8,128)} %bitcast.102), channel_id=1, source_target_pairs={{0,1},{1,2},{2,3},{3,4},{4,5},{5,6},{6,7},{7,8},{8,9},{9,10},{10,1... | collective-permute-start | bytes 19660808 | tf_op jit(solution)/shard_map/ppermute | solution.py:28
  648.5 173.1 %collective-permute-start.9 = (bf16[10,4096]{1,0:T(8,128)(2,1)S(1)}, bf16[10,4096]{1,0:T(8,128)(2,1)S(1)}, u32[]{:S(2)}, u32[]{:S(2)}) collective-permute-start(bf16[10,4096]{1,0:T(8,128)(2,1)S(1)} %copy-done.1), channel_id=1, source_target_pairs={{0,2},{1,3},{2,4},{3,5},{4,6},{5,7},{6,8},{7,9},{8,10},{9,11},{10,... | collective-permute-start | bytes 245768 | tf_op jit(solution)/shard_map/ppermute | solution.py:28
  650.4 171.2 %collective-permute-start.10 = (bf16[10,4096]{1,0:T(8,128)(2,1)S(1)}, bf16[10,4096]{1,0:T(8,128)(2,1)S(1)}, u32[]{:S(2)}, u32[]{:S(2)}) collective-permute-start(bf16[10,4096]{1,0:T(8,128)(2,1)S(1)} %copy-done.1), channel_id=1, source_target_pairs={{0,1},{1,2},{2,3},{3,4},{4,5},{5,6},{6,7},{7,8},{8,9},{9,10},{10,1... | collective-permute-start | bytes 245768 | tf_op jit(solution)/shard_map/ppermute | solution.py:19
  652.3 169.2 %collective-permute-start.11 = (bf16[10,4096]{1,0:T(8,128)(2,1)S(1)}, bf16[10,4096]{1,0:T(8,128)(2,1)S(1)}, u32[]{:S(2)}, u32[]{:S(2)}) collective-permute-start(bf16[10,4096]{1,0:T(8,128)(2,1)S(1)} %copy-done.1), channel_id=1, source_target_pairs={{1,0},{2,1},{3,2},{4,3},{5,4},{6,5},{7,6},{8,7},{9,8},{10,9},{11,1... | collective-permute-start | bytes 245768 | tf_op jit(solution)/shard_map/ppermute | solution.py:20
  660.2 135.5 %collective-permute-start.5 = (s32[10]{0:T(128)S(1)}, s32[10]{0:T(128)S(1)}, u32[]{:S(2)}, u32[]{:S(2)}) collective-permute-start(s32[10]{0:T(128)S(1)} %copy-done.3), channel_id=1, source_target_pairs={{0,2},{1,3},{2,4},{3,5},{4,6},{5,7},{6,8},{7,9},{8,10},{9,11},{10,... | collective-permute-start | bytes 128 | tf_op jit(solution)/shard_map/ppermute | solution.py:28
  795.7 9.1 collective-permute-start.6
  804.8 5.4 collective-permute-start.7
  810.2 6.9 collective-permute-start.8
  817.1 8.4 collective-permute-start.12
Sparse Core Ops, SparseCore 0:
  890.1 133.9 all-reduce.3
where the time goes:
time: 1040 us
  matrix products  466 us (45%)
  waiting for transfers between devices  298 us (29%)
  local copies, waits for them, and re-layouts  201 us (19%)
  starting transfers between devices  44.9 us (4%)
  between operations  14.5 us (1%)
  other arithmetic  11.6 us (1%)
    dot_general x10, matrix products, accumulate_block_entry(): jnp.einsum('rmt,rmqx->tqx', owner_hot, part, precision=highest_precision_...  298 us
    ppermute x5, waiting for transfers between devices, passed_along(): return lax.ppermute(array, axis, pairs)  142 us
    psum x1, waiting for transfers between devices, per_device(): level3 = lax.psum(share_sum, 'row')  134 us
    dot_general x10, matrix products, accumulate_block_entry(): jnp.einsum('rkfmq,rkmc->rfcq', prod, hot, precision=highest_precision_flag)  74.3 us
    dot_general x10, matrix products, accumulate_block_entry(): jnp.einsum('rfmq,rfx->rmqx', pmat, wide, preferred_element_type=jnp.float32)  67.9 us
    reshape x10, local copies, waits for them, and re-layouts, accumulate_block_entry(): prod = prod.reshape(prod.shape[0], KA, B, KP, B)  30.8 us
    gather x10, local copies, waits for them, and re-layouts, accumulate_block_entry(): prow = ext_p[local]  27.3 us
    ppermute x4, starting transfers between devices, padded(): after = lax.ppermute(leading, axis, down)  25.2 us
  transfers between devices with their start and end apart: 14, of which 8 were waited for; matrix products, arithmetic and copies ran while one was open for 2% of the time, Pallas kernels for 0%

commit v1 on v0

v1 whole, which is shorter than its diff:
```python
import functools

import jax
import jax.numpy as jnp
from jax import lax
from jax.experimental import pallas as pl
from jax.experimental.pallas import tpu as pltpu
from jax.sharding import Mesh
from jax.sharding import PartitionSpec as P

B = 64
KA = 8
KP = 4
A3G = 12
BR = 40
CR = 10
FR = BR * B
BAND = CR * B
L3 = A3G * B
RELAY = 11
BF = jnp.bfloat16
F32 = jnp.float32
SMEM = pl.BlockSpec(memory_space=pltpu.SMEM)
VMEM = pl.BlockSpec(memory_space=pltpu.VMEM)
ANY = pl.BlockSpec(memory_space=pl.ANY)
ROW = ("z", "x")
ALL = ("grp", "z", "x")


def kernel_params():
    return pltpu.CompilerParams(vmem_limit_bytes=56 << 20)


def cost(gflop, mbytes):
    return pl.CostEstimate(flops=gflop * 10**9, bytes_accessed=mbytes * 10**6, transcendentals=0)


def rows64(i):
    return pl.ds(pl.multiple_of(i * B, B), B)


def rows_at(start, height):
    return pl.ds(pl.multiple_of(start, height), height)


def half_of(shape):
    return lax.broadcasted_iota(jnp.int32, shape, 1) // B


def pta_kernel(cols, count, pcol, a_ref, p_ref, out_ref, acc):
    step = pl.program_id(0)
    pairs = acc.shape[0]
    height = out_ref.shape[1]
    some = height // B

    @pl.when(step == 0)
    def start():
        def clear(j, c):
            for q in range(pairs):
                acc[q, rows_at(j * 128, 128), :] = jnp.zeros((128, 128), F32)
            return c

        lax.fori_loop(0, 3 * BR // 2, clear, 0)

    @pl.when(step < BR // some)
    def accumulate():
        half = half_of((B, 2 * B))
        slot = lax.broadcasted_iota(jnp.int32, (KA * B, B), 0) // B

        def row(n, c):
            i = step * some + n
            r = rows64(i)
            at = a_ref[r, :].T
            at = jnp.where(slot < count[i], at, jnp.zeros_like(at))
            parts = []
            for m in range(KP):
                t = pcol[i, m]
                x = p_ref[r, (m // 2) * 128 : (m // 2) * 128 + 128]
                y = jnp.concatenate([x[:, B:], x[:, :B]], axis=1)
                x = jnp.where(t % 2 == m % 2, x, y)
                parts.append(jnp.where(half == t % 2, x, jnp.zeros_like(x)))
            rhs = jnp.concatenate(parts, axis=1)
            for k in range(KA):
                z = jnp.dot(at[k * B : k * B + B, :], rhs, preferred_element_type=F32)
                rr = rows64(cols[i, k])
                for m in range(KP):
                    acc[pcol[i, m] // 2, rr, :] += z[:, m * 128 : m * 128 + 128]
            return c

        lax.fori_loop(0, some, row, 0, unroll=2)

    base = step * height

    def finish(j, c):
        src = rows_at(base + j * 64, 64)
        dst = rows64(j)
        for q in range(pairs):
            o = (q % (pairs // 2)) * 128
            out_ref[q // (pairs // 2), dst, o : o + 128] = acc[q, src, :].astype(BF)
        return c

    lax.fori_loop(0, height // 64, finish, 0)


def pta(cols, count, pcol, a, p):
    steps = 12
    height = 3 * FR // steps
    return pl.pallas_call(
        pta_kernel,
        grid=(steps,),
        out_shape=jax.ShapeDtypeStruct((2, 3 * FR, BAND), BF),
        in_specs=[SMEM, SMEM, SMEM, VMEM, VMEM],
        out_specs=pl.BlockSpec((2, height, BAND), lambda s: (0, s, 0)),
        scratch_shapes=[pltpu.VMEM((CR, 3 * FR, 128), F32)],
        compiler_params=kernel_params(),
        cost_estimate=cost(12, 24),
        name="pta",
    )(cols, count, pcol, a, p)


def build_pt(wcol, p_ref, pt):
    def clear(j, c):
        pt[rows64(j), :] = jnp.zeros((B, FR), BF)
        return c

    lax.fori_loop(0, 2 * CR, clear, 0)
    half = half_of((B, 2 * B))

    def pair(jp, c):
        lanes = pl.ds(pl.multiple_of(jp * 128, 128), 128)
        xt = p_ref[lanes, :].T
        for n in range(KP):
            x = xt[n * B : n * B + B, :]
            for s in range(2):
                r = rows64(wcol[2 * jp + s, n])
                pt[r, lanes] = jnp.where(half == s, x, pt[r, lanes])
        return c

    lax.fori_loop(0, BR // 2, pair, 0)


def tiles(height, body):
    def tile(i, c):
        body(rows_at(i * 320, 320))
        return c

    lax.fori_loop(0, height // 320, tile, 0)


def shifted(r, by):
    return pl.ds(pl.multiple_of(r.start + by, 320), r.size)


def own_up_kernel(wcol, p_ref, pat_hbm, out_ref, pt, pat, sem):
    copy = pltpu.make_async_copy(pat_hbm.at[1, pl.ds(FR, FR), :], pat, sem)
    copy.start()
    build_pt(wcol, p_ref, pt)
    copy.wait()

    def body(r):
        out_ref[r, :] = jnp.dot(pt[r, :], pat[...], preferred_element_type=F32)

    tiles(2 * BAND, body)


def own_up(wcol, p, pat):
    return pl.pallas_call(
        own_up_kernel,
        out_shape=jax.ShapeDtypeStruct((2 * BAND, BAND), F32),
        in_specs=[SMEM, VMEM, ANY],
        out_specs=VMEM,
        scratch_shapes=[
            pltpu.VMEM((2 * BAND, FR), BF),
            pltpu.VMEM((FR, BAND), BF),
            pltpu.SemaphoreType.DMA,
        ],
        compiler_params=kernel_params(),
        cost_estimate=cost(4, 8),
        name="own_up",
    )(wcol, p, pat)


def halo_up_kernel(part, wcol, p_ref, pat_hbm, own_ref, out_ref, pt, pat, sem):
    copy = pltpu.make_async_copy(pat_hbm.at[1, pl.ds(part * FR, FR), :], pat, sem)
    copy.start()
    build_pt(wcol, p_ref, pt)
    copy.wait()

    def body(r):
        z = jnp.dot(pt[r, :], pat[...], preferred_element_type=F32)
        out_ref[r, :] = z.astype(BF)

    def shared(r):
        r = shifted(r, BAND if part == 0 else 0)
        own = own_ref[shifted(r, -BAND if part == 0 else BAND), :]
        z = jnp.dot(pt[r, :], pat[...], preferred_element_type=F32) + own
        out_ref[r, :] = z.astype(BF)

    def alone(r):
        body(shifted(r, 0 if part == 0 else BAND))

    tiles(BAND, alone)
    tiles(BAND, shared)


def halo_up(part, wcol, p, pat, own):
    return pl.pallas_call(
        functools.partial(halo_up_kernel, part),
        out_shape=jax.ShapeDtypeStruct((2 * BAND, BAND), BF),
        in_specs=[SMEM, VMEM, ANY, VMEM],
        out_specs=VMEM,
        scratch_shapes=[
            pltpu.VMEM((2 * BAND, FR), BF),
            pltpu.VMEM((FR, BAND), BF),
            pltpu.SemaphoreType.DMA,
        ],
        compiler_params=kernel_params(),
        cost_estimate=cost(4, 10),
        name=f"halo_up{part}",
    )(wcol, p, pat, own)


def low_kernel(wlow, wcol, whigh, plow, p_ref, phigh, pat_hbm, out_ref, pt, acc, pat, sems):
    copies = [
        pltpu.make_async_copy(pat_hbm.at[0, pl.ds(part * FR, FR), :], pat.at[part], sems.at[part])
        for part in range(3)
    ]
    for copy in copies:
        copy.start()
    build_pt(wcol, p_ref, pt)
    copies[1].wait()

    def middle(r):
        acc[r, :] = jnp.dot(pt[r, :], pat[1], preferred_element_type=F32)

    tiles(2 * BAND, middle)
    for part, w, p, start, mine in ((0, wlow, plow, 0, -BAND), (2, whigh, phigh, 2 * BAND, BAND)):
        build_pt(w, p, pt)
        copies[part].wait()

        def alone(r):
            r = shifted(r, 0 if part == 0 else BAND)
            z = jnp.dot(pt[r, :], pat[part], preferred_element_type=F32)
            out_ref[shifted(r, start), :] = z.astype(BF)

        def shared(r):
            r = shifted(r, BAND if part == 0 else 0)
            z = jnp.dot(pt[r, :], pat[part], preferred_element_type=F32) + acc[shifted(r, mine), :]
            out_ref[shifted(r, start), :] = z.astype(BF)

        tiles(BAND, alone)
        tiles(BAND, shared)


def low_rows(wlow, wcol, whigh, plow, p, phigh, pat):
    return pl.pallas_call(
        low_kernel,
        out_shape=jax.ShapeDtypeStruct((4 * BAND, BAND), BF),
        in_specs=[SMEM] * 3 + [VMEM] * 3 + [ANY],
        out_specs=VMEM,
        scratch_shapes=[
            pltpu.VMEM((2 * BAND, FR), BF),
            pltpu.VMEM((2 * BAND, BAND), F32),
            pltpu.VMEM((3, FR, BAND), BF),
            pltpu.SemaphoreType.DMA((3,)),
        ],
        compiler_params=kernel_params(),
        cost_estimate=cost(13, 18),
        name="low_rows",
    )(wlow, wcol, whigh, plow, p, phigh, pat)


def level3_kernel(mine, flags, agg, q_ref, *refs):
    parts, outs, qt, u = refs[:-4], refs[-4:-2], refs[-2], refs[-1]
    half = half_of((B, 2 * B))
    qt[...] = jnp.zeros_like(qt)
    for s in range(4):
        for cp in range(CR // 2):
            x = q_ref[s, cp * 128 : cp * 128 + 128, :].T
            for e in range(2):
                r = rows64(agg[s, 2 * cp + e])
                lanes = slice(cp * 128, cp * 128 + 128)
                qt[s, r, lanes] = jnp.where(half == e, x, qt[s, r, lanes])
    u[...] = jnp.zeros_like(u)
    for n, part in enumerate(parts):
        count = 4 // len(parts)

        def expand(s, c):
            here = part[rows_at(s * BAND, BAND), :]
            s = s + n * count
            u[flags[s]] += jnp.dot(qt[s], here, preferred_element_type=F32)
            return c

        lax.fori_loop(0, count, expand, 0)

    def finish(to):
        z = lax.dot_general(
            u[to].astype(BF), qt[mine], (((1,), (1,)), ((), ())), preferred_element_type=F32
        )
        outs[to][...] = z.T.astype(BF)

    finish(0)
    pl.when(flags[4] == 1)(lambda: finish(1))

    @pl.when(flags[4] == 0)
    def empty():
        outs[1][...] = jnp.zeros((L3, L3), BF)


def level3_parts(mine, flags, agg, q, *parts):
    return pl.pallas_call(
        functools.partial(level3_kernel, mine),
        out_shape=[jax.ShapeDtypeStruct((L3, L3), BF)] * 2,
        in_specs=[SMEM, SMEM, VMEM] + [VMEM] * len(parts),
        out_specs=[VMEM] * 2,
        scratch_shapes=[pltpu.VMEM((4, L3, BAND), BF), pltpu.VMEM((2, L3, BAND), F32)],
        compiler_params=kernel_params(),
        cost_estimate=cost(3, 6),
        name=f"level3_parts{mine}",
    )(flags, agg, q, *parts)


def level2_kernel(low, got_a, got_b, out_ref):
    s = pl.program_id(0)
    mine = jnp.where(s >= 1, low[...].T.astype(F32), 0.0)
    got = jnp.where(s <= 1, got_a[...], got_b[...])
    theirs = jnp.where(s <= 3, got.T.astype(F32), 0.0)
    out_ref[...] = (mine + theirs).astype(BF)


def level2_rows(rt, got_a, got_b):
    return pl.pallas_call(
        level2_kernel,
        grid=(5,),
        out_shape=jax.ShapeDtypeStruct((BAND, 5 * BAND), BF),
        in_specs=[
            pl.BlockSpec((BAND, BAND), lambda s: (jnp.maximum(s - 1, 0), 0)),
            pl.BlockSpec((BAND, BAND), lambda s: (jnp.minimum(s, 1), 0)),
            pl.BlockSpec((BAND, BAND), lambda s: (jnp.clip(s - 2, 0, 1), 0)),
        ],
        out_specs=pl.BlockSpec((BAND, BAND), lambda s: (0, s)),
        compiler_params=kernel_params(),
        cost_estimate=cost(1, 14),
        name="level2_rows",
    )(rt, got_a, got_b)


def place_kernel(z, own, below, above, far_a, far_b, out_ref):
    g = pl.program_id(0)
    cut = far_a.shape[0]

    @pl.when(g == 0)
    def here():
        out_ref[...] = own[...].astype(F32)

    @pl.when(g == 1)
    def next_one():
        out_ref[...] = above[...].astype(F32)

    @pl.when(g == 2)
    def opposite():
        out_ref[:cut, :] = far_a[...].astype(F32)
        out_ref[cut:, :] = far_b[...].astype(F32)

    @pl.when(g == 3)
    def previous():
        out_ref[...] = below[...].astype(F32)


def place(z, own, below, above, far_a, far_b):
    height, width = own.shape
    return pl.pallas_call(
        place_kernel,
        grid_spec=pltpu.PrefetchScalarGridSpec(
            num_scalar_prefetch=1,
            grid=(4,),
            in_specs=[VMEM] * 5,
            out_specs=pl.BlockSpec((height, width), lambda g, z: ((z[0] + g) % 4, 0)),
        ),
        out_shape=jax.ShapeDtypeStruct((4 * height, width), F32),
        compiler_params=kernel_params(),
        cost_estimate=cost(1, 11),
        name="place",
    )(z, own, below, above, far_a, far_b)


def moved(array, by):
    devices = lax.axis_size(ALL)
    pairs = [(i, i + by) for i in range(devices) if 0 <= i + by < devices]
    return lax.ppermute(array, ALL, pairs)


def per_device(a_blocks, a_cols, a_count, p_blocks, p_cols, q2_blocks, agg3):
    row_size = lax.axis_size(ROW)
    sz, sx = lax.axis_size("z"), lax.axis_size("x")
    groups = lax.axis_size("grp")
    device = lax.axis_index(ALL)
    row = lax.axis_index(ROW)
    wcol = p_cols - device * CR
    cols = a_cols - (device - 1) * BR
    slot3 = agg3 % A3G

    width = KP * B
    q_rows = BAND * B // width
    small = jnp.concatenate([wcol.reshape(-1), slot3, jnp.zeros((width - BR * KP - CR,), jnp.int32)])
    small = jnp.pad(small.astype(BF)[None], ((0, 15), (0, 0)))
    tail = jnp.concatenate([q2_blocks.reshape(q_rows, width), small], axis=0)
    mine = jnp.concatenate([p_blocks, tail], axis=0)
    lower = moved(mine, 1)
    higher = moved(mine, -1)

    def numbers(t):
        return t[q_rows].astype(jnp.int32)

    def window(t):
        return numbers(t)[: BR * KP].reshape(BR, KP)

    pat = pta(cols, a_count, wcol, a_blocks, p_blocks)
    tail, pat = lax.optimization_barrier((tail, pat))
    far = moved(tail, -2)
    own = own_up(wcol, p_blocks, pat)
    wlow, whigh = window(lower[FR:]), window(higher[FR:])
    up_a = halo_up(0, wlow, lower, pat, own)
    got_a = moved(up_a, 1)
    up_b = halo_up(2, whigh, higher, pat, own)
    got_b = moved(up_b, 1)
    tails = jnp.stack([lower[FR:], tail, higher[FR:], far])
    q = tails[:, :q_rows].reshape(4, BAND, B)
    agg = tails[:, q_rows, BR * KP : BR * KP + CR].astype(jnp.int32)
    first, last = row == 0, row == row_size - 1
    ahead = row + 2 >= row_size
    flags = jnp.stack([first, row < 0, last, ahead, first | ahead]).astype(jnp.int32)
    upper_c, upper_s = level3_parts(2, flags, agg, q, up_a, up_b)

    def over(to):
        return [(g * row_size + row_size - 1, (g + 1) * row_size + to) for g in range(groups - 1)]

    late_s = lax.ppermute(upper_c, ALL, over(RELAY))
    late_c = lax.ppermute(upper_s, ALL, over(row_size - 1))
    wlow, upper_c = lax.optimization_barrier((wlow, upper_c))
    low = low_rows(wlow, wcol, whigh, lower, p_blocks, higher, pat)
    low, got_b = lax.optimization_barrier((low, got_b))
    lower_c, lower_s = level3_parts(1, flags, agg, q, low)
    lower_c, got_a = lax.optimization_barrier((lower_c, got_a))

    def total(lower_part, upper_part, late):
        upper_part = jnp.where(last, 0.0, upper_part.astype(F32))
        return (lower_part.astype(F32) + upper_part + late.astype(F32)).astype(BF)

    main = jnp.concatenate([total(lower_c, upper_c, late_c), total(lower_s, upper_s, late_s)], axis=1)

    chunk = L3 // row_size
    part = lax.all_to_all(main, ROW, 0, 0, tiled=True).reshape(row_size, chunk, 2 * L3)
    left = part[0, :, L3:].astype(F32) + part[RELAY, :, L3:].astype(F32)
    right = part[row_size - 2, :, L3:].astype(F32) + part[row_size - 1, :, L3:].astype(F32)
    middle = jnp.sum(part[:, :, :L3].astype(F32), axis=0)
    whole = jnp.concatenate([left, middle, right], axis=1).astype(BF)

    whole = lax.all_to_all(jnp.tile(whole, (sx, 1)), "x", 0, 0, tiled=True)
    tall = L3 // sz
    onward = [(i, (i + 1) % sz) for i in range(sz)]
    back = [(i, (i - 1) % sz) for i in range(sz)]
    below = lax.ppermute(whole, "z", onward)
    above = lax.ppermute(whole, "z", back)
    far_a = lax.ppermute(below[: tall // 2], "z", onward)
    far_b = lax.ppermute(above[tall // 2 :], "z", back)
    z = lax.axis_index("z").astype(jnp.int32)[None]
    level3 = place(z, whole, below, above, far_a, far_b)
    level2 = level2_rows(low, got_a, got_b)
    return (level2, level3)


def solution(mesh):
    grp, row = mesh.devices.shape
    fine = Mesh(mesh.devices.reshape(grp, 4, row // 4), ALL)
    in_specs = (P(ALL, None), P(ALL, None), P(ALL), P(ALL, None), P(ALL, None), P(ALL, None), P(ALL))
    out_specs = (P(ALL, None), P("grp", None))
    return jax.shard_map(
        per_device, mesh=fine, in_specs=in_specs, out_specs=out_specs, check_vma=False
    )
```

time: 1040 us -> 253 us (0.24)
  matrix products: 466 us -> 0 us
  waiting for transfers between devices: 298 us -> 20.5 us
  local copies, waits for them, and re-layouts: 201 us -> 9.24 us
  Pallas kernels: 0 us -> 126 us
  blocking collectives: 0 us -> 55.9 us
  starting transfers between devices: 44.9 us -> 28.6 us
  between operations: 14.5 us -> 0.96 us
    dot_general x44 -> x0, matrix products: 466 us -> none  [the longest x10 298 us: accumulate_block_entry(): jnp.einsum('rmt,rmqx->tqx', owner_hot, part, precision=highest_precision_...]
    ppermute x13 -> x11, waiting for transfers between devices: 164 us -> 20.5 us  [the longest x1 17.7 us: per_device(): above = lax.ppermute(whole, 'z', back)]
    psum x1 -> x0, waiting for transfers between devices: 134 us -> none  [per_device(): level3 = lax.psum(share_sum, 'row')]
    pallas_call x0 -> x9, Pallas kernels: none -> 126 us  [the longest x1 28.9 us: low_rows(): pl.pallas_call(low_kernel, out_shape=jax.ShapeDtypeStruct((4 * BAND, BAND...]
    reshape x26 -> x2, local copies, waits for them, and re-layouts: 78.1 us -> 3.14 us  [the longest x1 2.17 us: per_device(): q = tails[:, :q_rows].reshape(4, BAND, B)]
    all_to_all x0 -> x2, blocking collectives: none -> 55.9 us  [the longest x1 40.8 us: per_device(): lax.all_to_all(main, ROW, 0, 0, tiled=True).reshape(row_size, chunk, 2 * L3)]
    gather x20 -> x0, local copies, waits for them, and re-layouts: 33 us -> none  [the longest x10 27.3 us: accumulate_block_entry(): prow = ext_p[local]]
    dynamic_slice x30 -> x0, local copies, waits for them, and re-layouts: 23.2 us -> none  [per_device(): lax.scan(accumulate_block_entry, start, (blk_a, blk_cols, blk_count, blk_...]
  transfers between devices with their start and end apart: 14 -> 11, of which waited for: 8 -> 2; matrix products, arithmetic and copies ran while one was open for 2% -> 5% of each run, Pallas kernels for 0% -> 48%
where the time goes in v1:
time: 253 us
  Pallas kernels  126 us (50%)
  blocking collectives  55.9 us (22%)
  starting transfers between devices  28.6 us (11%)
  waiting for transfers between devices  20.5 us (8%)
  other arithmetic  11.7 us (5%)
  local copies, waits for them, and re-layouts  9.24 us (4%)
    all_to_all x1, blocking collectives, per_device(): lax.all_to_all(main, ROW, 0, 0, tiled=True).reshape(row_size, chunk, 2 * L3)  40.8 us
    pallas_call x1, Pallas kernels, low_rows(): pl.pallas_call(low_kernel, out_shape=jax.ShapeDtypeStruct((4 * BAND, BAND...  28.9 us
    pallas_call x1, Pallas kernels, pta(): pl.pallas_call(pta_kernel, grid=(steps,), out_shape=jax.ShapeDtypeStruct(...  27.3 us
    pallas_call x2, Pallas kernels, halo_up(): pl.pallas_call(functools.partial(halo_up_kernel, part), out_shape=jax.Sha...  23.5 us
    pallas_call x2, Pallas kernels, level3_parts(): pl.pallas_call(functools.partial(level3_kernel, mine), out_shape=[jax.Sha...  22.6 us
    ppermute x5, starting transfers between devices, moved(): return lax.ppermute(array, ALL, pairs)  21.9 us
    ppermute x1, waiting for transfers between devices, per_device(): above = lax.ppermute(whole, 'z', back)  17.7 us
    all_to_all x1, blocking collectives, per_device(): whole = lax.all_to_all(jnp.tile(whole, (sx, 1)), 'x', 0, 0, tiled=True)  15.1 us
  transfers between devices with their start and end apart: 11, of which 2 were waited for; matrix products, arithmetic and copies ran while one was open for 5% of the time, Pallas kernels for 48%

profile of v1, /device:TPU:8, one launch (start us, length us, event | category | flops | bytes accessed | tf_op | source)
XLA Modules:
  0.0 252.7 jit_solution(4423995758667533362)
XLA Ops:
  3.0 1.0 reshape.108
  3.9 2.5 pad_maximum_fusion.1
  6.4 7.5 %collective-permute-start.1 = (bf16[2736,256]{1,0:T(8,128)(2,1)}, bf16[2736,256]{1,0:T(8,128)(2,1)S(1)}, u32[]{:S(2)}, u32[]{:S(2)}) collective-permute-start(bf16[2736,256]{1,0:T(8,128)(2,1)} %pad_maximum_fusion.1), channel_id=1, source_target_pairs={{1,0},{2,1},{3,2},{4,3},{5,4},{6,5},{7,6},{8,7},{9,8},{10,9},{11,1... | collective-permute-start | bytes 4202504 | tf_op jit(solution)/shard_map/ppermute | solution.py:390
  13.9 1.9 collective-permute-start
  16.5 27.3 %pta.1.pat_hbm = bf16[2,7680,640]{2,1,0:T(8,128)(2,1)} custom-call(s32[40,8]{1,0:T(8,128)} %broadcast_subtract_fusion.cols, s32[40]{0:T(128)} %count.1, s32[40,4]{1,0:T(8,128)} %get-tuple-element.27.pcol.wcol, bf16[2560,512]{1,0:T(8,128)(2,1)} %a_ref.1, bf16[2560,256]{1,0:T(8,128)(2,1)} %p_ref.5), custom_call_target="tpu_custom_call" | custom-call | flops 12000000000 | bytes 24000000 | tf_op jit(solution)/shard_map/pta/pallas_call | solution.py:108
  43.8 3.6 %collective-permute-start.2 = (bf16[176,256]{1,0:T(8,128)(2,1)S(1)}, bf16[176,256]{1,0:T(8,128)(2,1)}, u32[]{:S(2)}, u32[]{:S(2)}) collective-permute-start(bf16[176,256]{1,0:T(8,128)(2,1)S(1)} %pad_maximum_fusion.6), channel_id=1, source_target_pairs={{2,0},{3,1},{4,2},{5,3},{6,4},{7,5},{8,6},{9,7},{10,8},{11,9},{12,... | collective-permute-start | bytes 270344 | tf_op jit(solution)/shard_map/ppermute | solution.py:390
  48.1 11.2 %own_up.1.own_ref = f32[1280,640]{1,0:T(8,128)} custom-call(s32[40,4]{1,0:T(8,128)} %get-tuple-element.27.pcol.wcol, bf16[2560,256]{1,0:T(8,128)(2,1)} %p_ref.5, bf16[2,7680,640]{2,1,0:T(8,128)(2,1)} %pta.1.pat_hbm), custom_call_target="tpu_custom_call" | custom-call | flops 4000000000 | bytes 8000000 | tf_op jit(solution)/shard_map/own_up/pallas_call | solution.py:167
  59.4 0.9 reshape.112.wcol.whigh
  60.3 0.9 reshape.110.wcol.wlow
  61.4 11.8 %halo_up2.1.refs_1_ = bf16[1280,640]{1,0:T(8,128)(2,1)} custom-call(s32[40,4]{1,0:T(8,128)} %reshape.112.wcol.whigh, bf16[2736,256]{1,0:T(8,128)(2,1)} %copy-done.6, bf16[2,7680,640]{2,1,0:T(8,128)(2,1)} %pta.1.pat_hbm, f32[1280,640]{1,0:T(8,128)} %own_up.1.own_ref), custom_call_target="tpu_custom_call" | custom-call | flops 4000000000 | bytes 10000000 | tf_op jit(solution)/shard_map/halo_up2/pallas_call | solution.py:207
  73.2 7.0 %collective-permute-start.3 = (bf16[1280,640]{1,0:T(8,128)(2,1)}, bf16[1280,640]{1,0:T(8,128)(2,1)S(1)}, u32[]{:S(2)}, u32[]{:S(2)}) collective-permute-start(bf16[1280,640]{1,0:T(8,128)(2,1)} %halo_up2.1.refs_1_), channel_id=1, source_target_pairs={{0,1},{1,2},{2,3},{3,4},{4,5},{5,6},{6,7},{7,8},{8,9},{9,10},{10,1... | collective-permute-start | bytes 4915208 | tf_op jit(solution)/shard_map/ppermute | solution.py:390
  80.2 0.9 slice_bitcast_fusion
  81.1 11.7 %halo_up0.1.refs_0_ = bf16[1280,640]{1,0:T(8,128)(2,1)} custom-call(s32[40,4]{1,0:T(8,128)} %reshape.110.wcol.wlow, bf16[2736,256]{1,0:T(8,128)(2,1)} %copy-done.7, bf16[2,7680,640]{2,1,0:T(8,128)(2,1)} %pta.1.pat_hbm, f32[1280,640]{1,0:T(8,128)} %own_up.1.own_ref), custom_call_target="tpu_custom_call" | custom-call | flops 4000000000 | bytes 10000000 | tf_op jit(solution)/shard_map/halo_up0/pallas_call | solution.py:207
  92.8 1.0 slice_bitcast_fusion.1
  93.9 1.6 pad_maximum_fusion.2
  95.5 2.2 reshape.109.q_ref
  97.7 1.9 collective-permute-start.4
  99.6 1.3 maximum_convert_fusion
  100.9 11.1 %level3_parts2.1 = (bf16[768,768]{1,0:T(8,128)(2,1)}, bf16[768,768]{1,0:T(8,128)(2,1)}) custom-call(s32[5]{0:T(128)} %convert_element_type.80.flags, s32[4,10]{1,0:T(4,128)} %bitcast.27, bf16[4,640,64]{2,1,0:T(8,128)(2,1)} %reshape.109.q_ref, bf16[1280,640]{1,0:T(8,128)(2,1)} %halo_up0.1.refs_0_, bf16[1280,640]{1,0:T(8,128)(2,1)} %halo_up2.1.refs_1_), custom_call_target="tpu_custom_call" | custom-call | flops 3000000000 | bytes 6000000 | tf_op jit(solution)/shard_map/level3_parts2/pallas_call | solution.py:311
  112.0 1.8 collective-permute-start.6
  114.5 28.9 %low_rows.1.refs_0_.low = bf16[2560,640]{1,0:T(8,128)(2,1)} custom-call(s32[40,4]{1,0:T(8,128)} %reshape.110.wcol.wlow, s32[40,4]{1,0:T(8,128)} %get-tuple-element.27.pcol.wcol, s32[40,4]{1,0:T(8,128)} %reshape.112.wcol.whigh, bf16[2736,256]{1,0:T(8,128)(2,1)} %copy-done.7, bf16[2560,256]{1,0:T(8,128)(2,1)} %p_ref.5, bf16[2736,256]{1,0:T(8,128)(2,1)} %copy-done.6, ...), custom_call_target="tpu_custom_call" | custom-call | flops 12999999488 | bytes 18000000 | tf_op jit(solution)/shard_map/low_rows/pallas_call | solution.py:256
  143.5 11.4 %level3_parts1.1 = (bf16[768,768]{1,0:T(8,128)(2,1)}, bf16[768,768]{1,0:T(8,128)(2,1)}) custom-call(s32[5]{0:T(128)} %convert_element_type.80.flags, s32[4,10]{1,0:T(4,128)} %bitcast.28, bf16[4,640,64]{2,1,0:T(8,128)(2,1)} %reshape.109.q_ref, bf16[2560,640]{1,0:T(8,128)(2,1)} %low_rows.1.refs_0_.low), custom_call_target="tpu_custom_call" | custom-call | flops 3000000000 | bytes 6000000 | tf_op jit(solution)/shard_map/level3_parts1/pallas_call | solution.py:311
  155.0 2.7 %add_convert_fusion = bf16[768,768]{1,0:T(8,128)(2,1)S(1)} fusion(bf16[768,768]{1,0:T(8,128)(2,1)} %collective-permute-done.6, bf16[768,768]{1,0:T(8,128)(2,1)S(1)} %copy-done.9, bf16[768,768]{1,0:T(8,128)(2,1)} %get-tuple-element.25, pred[]{:T(512)} %eq.9), kind=kLoop, calls=%fused_computation.1 | loop fusion | flops 4128768 | bytes 4718593 | tf_op jit(solution)/shard_map/convert_element_type | solution.py:448
  158.6 40.8 %all_to_all.17 = bf16[16,48,1536]{2,1,0:T(8,128)(2,1)S(1)} all-to-all(bf16[16,48,1536]{2,1,0:T(8,128)(2,1)S(1)} %bitcast.21), channel_id=1, replica_groups=mesh['grp'=8,'z'=4,'x'=4] {'z','x'}, dimensions={0} | all-to-all | bytes 4718592 | tf_op jit(solution)/shard_map/all_to_all | solution.py:453
  199.8 15.1 %all_to_all.18 = bf16[4,48,2304]{2,1,0:T(8,128)(2,1)S(1)} all-to-all(bf16[4,48,2304]{2,1,0:T(8,128)(2,1)S(1)} %tile.2), channel_id=1, replica_groups=mesh['grp'=8,'z'=4,'x'=4] {'x'}, dimensions={0} | all-to-all | bytes 1769472 | tf_op jit(solution)/shard_map/all_to_all | solution.py:459
  214.9 0.9 collective-permute-start.8
  215.7 1.2 collective-permute-start.7
  216.9 17.7 %collective-permute-done.8.above = bf16[192,2304]{1,0:T(8,128)(2,1)S(1)} collective-permute-done((bf16[192,2304]{1,0:T(8,128)(2,1)S(1)}, bf16[192,2304]{1,0:T(8,128)(2,1)S(1)}, u32[]{:S(2)}, u32[]{:S(2)}) %collective-permute-start.8) | collective-permute-done | bytes 884768 | tf_op jit(solution)/shard_map/ppermute | solution.py:464
  234.6 2.0 collective-permute-start.10
  236.8 7.1 %level2_rows.1 = bf16[640,3200]{1,0:T(8,128)(2,1)} custom-call(bf16[2560,640]{1,0:T(8,128)(2,1)} %low_rows.1.refs_0_.low, bf16[1280,640]{1,0:T(8,128)(2,1)} %copy-done.5, bf16[1280,640]{1,0:T(8,128)(2,1)} %copy-done.4), custom_call_target="tpu_custom_call" | custom-call | flops 1000000000 | bytes 14000000 | tf_op jit(solution)/shard_map/level2_rows/pallas_call | solution.py:332
  244.0 2.8 %collective-permute-done.9.far_a = bf16[96,2304]{1,0:T(8,128)(2,1)S(1)} collective-permute-done((bf16[96,2304]{1,0:T(8,128)(2,1)S(1)}, bf16[96,2304]{1,0:T(8,128)(2,1)S(1)}, u32[]{:S(2)}, u32[]{:S(2)}) %collective-permute-start.9) | collective-permute-done | bytes 442400 | tf_op jit(solution)/shard_map/ppermute | solution.py:465
  247.5 5.2 %place.1 = f32[768,2304]{1,0:T(8,128)} custom-call(s32[1]{0:T(128)} %bitcast.11.z, bf16[192,2304]{1,0:T(8,128)(2,1)} %bitcast.24, bf16[192,2304]{1,0:T(8,128)(2,1)} %copy-done.2, bf16[192,2304]{1,0:T(8,128)(2,1)} %copy-done.1, bf16[96,2304]{1,0:T(8,128)(2,1)} %copy-done.12, bf16[96,2304]{1,0:T(8,128)(2,1)} %copy-done.11), custom_call_target="tpu_custom_call" | custom-call | flops 1000000000 | bytes 11000000 | tf_op jit(solution)/shard_map/place/pallas_call | solution.py:372
  (62 shorter events, 6.9 us)
Async XLA Ops:
  2.1 13.8 %copy-start.13 = (s32[40,8]{0,1:T(8,128)S(1)}, s32[40,8]{0,1:T(8,128)}, u32[]{:S(2)}) copy-start(s32[40,8]{0,1:T(8,128)} %param.8) | copy-start | bytes 3844
  6.4 53.0 %collective-permute-start.1 = (bf16[2736,256]{1,0:T(8,128)(2,1)}, bf16[2736,256]{1,0:T(8,128)(2,1)S(1)}, u32[]{:S(2)}, u32[]{:S(2)}) collective-permute-start(bf16[2736,256]{1,0:T(8,128)(2,1)} %pad_maximum_fusion.1), channel_id=1, source_target_pairs={{1,0},{2,1},{3,2},{4,3},{5,4},{6,5},{7,6},{8,7},{9,8},{10,9},{11,1... | collective-permute-start | bytes 4202504 | tf_op jit(solution)/shard_map/ppermute | solution.py:390
  13.9 46.4 %collective-permute-start = (bf16[2736,256]{1,0:T(8,128)(2,1)}, bf16[2736,256]{1,0:T(8,128)(2,1)S(1)}, u32[]{:S(2)}, u32[]{:S(2)}) collective-permute-start(bf16[2736,256]{1,0:T(8,128)(2,1)} %pad_maximum_fusion.1), channel_id=1, source_target_pairs={{0,1},{1,2},{2,3},{3,4},{4,5},{5,6},{6,7},{7,8},{8,9},{9,10},{10,1... | collective-permute-start | bytes 4202504 | tf_op jit(solution)/shard_map/ppermute | solution.py:390
  43.8 50.0 %collective-permute-start.2 = (bf16[176,256]{1,0:T(8,128)(2,1)S(1)}, bf16[176,256]{1,0:T(8,128)(2,1)}, u32[]{:S(2)}, u32[]{:S(2)}) collective-permute-start(bf16[176,256]{1,0:T(8,128)(2,1)S(1)} %pad_maximum_fusion.6), channel_id=1, source_target_pairs={{2,0},{3,1},{4,2},{5,3},{6,4},{7,5},{8,6},{9,7},{10,8},{11,9},{12,... | collective-permute-start | bytes 270344 | tf_op jit(solution)/shard_map/ppermute | solution.py:390
  59.4 1.8 copy-start.6
  60.3 1.2 copy-start.7
  73.2 70.3 %collective-permute-start.3 = (bf16[1280,640]{1,0:T(8,128)(2,1)}, bf16[1280,640]{1,0:T(8,128)(2,1)S(1)}, u32[]{:S(2)}, u32[]{:S(2)}) collective-permute-start(bf16[1280,640]{1,0:T(8,128)(2,1)} %halo_up2.1.refs_1_), channel_id=1, source_target_pairs={{0,1},{1,2},{2,3},{3,4},{4,5},{5,6},{6,7},{7,8},{8,9},{9,10},{10,1... | collective-permute-start | bytes 4915208 | tf_op jit(solution)/shard_map/ppermute | solution.py:390
  92.8 4.8 %copy-start.3 = (bf16[1280,640]{1,0:T(8,128)(2,1)S(1)}, bf16[1280,640]{1,0:T(8,128)(2,1)}, u32[]{:S(2)}) copy-start(bf16[1280,640]{1,0:T(8,128)(2,1)} %halo_up0.1.refs_0_) | copy-start | bytes 4915204
  97.7 57.2 %collective-permute-start.4 = (bf16[1280,640]{1,0:T(8,128)(2,1)S(1)}, bf16[1280,640]{1,0:T(8,128)(2,1)S(1)}, u32[]{:S(2)}, u32[]{:S(2)}) collective-permute-start(bf16[1280,640]{1,0:T(8,128)(2,1)S(1)} %copy-done.3), channel_id=1, source_target_pairs={{0,1},{1,2},{2,3},{3,4},{4,5},{5,6},{6,7},{7,8},{8,9},{9,10},{10,1... | collective-permute-start | bytes 4915208 | tf_op jit(solution)/shard_map/ppermute | solution.py:390
  112.0 42.9 %collective-permute-start.6 = (bf16[768,768]{1,0:T(8,128)(2,1)}, bf16[768,768]{1,0:T(8,128)(2,1)}, u32[]{:S(2)}, u32[]{:S(2)}) collective-permute-start(bf16[768,768]{1,0:T(8,128)(2,1)} %get-tuple-element.23), channel_id=1, source_target_pairs={{15,27},{31,43},{47,59},{63,75},{79,91},{95,107},{111,123}} | collective-permute-start | bytes 3538952 | tf_op jit(solution)/shard_map/ppermute | solution.py:438
  113.8 44.0 %collective-permute-start.5 = (bf16[768,768]{1,0:T(8,128)(2,1)}, bf16[768,768]{1,0:T(8,128)(2,1)S(1)}, u32[]{:S(2)}, u32[]{:S(2)}) collective-permute-start(bf16[768,768]{1,0:T(8,128)(2,1)} %get-tuple-element.24), channel_id=1, source_target_pairs={{15,31},{31,47},{47,63},{63,79},{79,95},{95,111},{111,127}} | collective-permute-start | bytes 3538952 | tf_op jit(solution)/shard_map/ppermute | solution.py:439
  143.4 11.5 %copy-start.9 = (bf16[768,768]{1,0:T(8,128)(2,1)S(1)}, bf16[768,768]{1,0:T(8,128)(2,1)}, u32[]{:S(2)}) copy-start(bf16[768,768]{1,0:T(8,128)(2,1)} %get-tuple-element.24) | copy-start | bytes 3538948
  143.5 11.5 %copy-start.4 = (bf16[1280,640]{1,0:T(8,128)(2,1)}, bf16[1280,640]{1,0:T(8,128)(2,1)S(1)}, u32[]{:S(2)}) copy-start(bf16[1280,640]{1,0:T(8,128)(2,1)S(1)} %collective-permute-done.3.got_b) | copy-start | bytes 4915204
  154.9 2.8 %copy-start.5 = (bf16[1280,640]{1,0:T(8,128)(2,1)}, bf16[1280,640]{1,0:T(8,128)(2,1)S(1)}, u32[]{:S(2)}) copy-start(bf16[1280,640]{1,0:T(8,128)(2,1)S(1)} %collective-permute-done.4.got_a) | copy-start | bytes 4915204
  155.0 2.8 %copy-start.8 = (bf16[768,768]{1,0:T(8,128)(2,1)S(1)}, bf16[768,768]{1,0:T(8,128)(2,1)}, u32[]{:S(2)}) copy-start(bf16[768,768]{1,0:T(8,128)(2,1)} %get-tuple-element.23) | copy-start | bytes 3538948
  155.0 2.9 %copy-start.10 = (bf16[768,768]{1,0:T(8,128)(2,1)S(1)}, bf16[768,768]{1,0:T(8,128)(2,1)}, u32[]{:S(2)}) copy-start(bf16[768,768]{1,0:T(8,128)(2,1)} %get-tuple-element.22) | copy-start | bytes 3538948
  214.9 29.1 %copy-start = (bf16[4,48,2304]{2,1,0:T(8,128)(2,1)}, bf16[4,48,2304]{2,1,0:T(8,128)(2,1)S(1)}, u32[]{:S(2)}) copy-start(bf16[4,48,2304]{2,1,0:T(8,128)(2,1)S(1)} %all_to_all.18) | copy-start | bytes 2654212
  214.9 19.7 %collective-permute-start.8 = (bf16[192,2304]{1,0:T(8,128)(2,1)S(1)}, bf16[192,2304]{1,0:T(8,128)(2,1)S(1)}, u32[]{:S(2)}, u32[]{:S(2)}) collective-permute-start(bf16[192,2304]{1,0:T(8,128)(2,1)S(1)} %bitcast.22), channel_id=1, source_target_pairs={{0,12},{4,0},{8,4},{12,8},{1,13},{5,1},{9,5},{13,9},{2,14},{6,2},{... | collective-permute-start | bytes 2654216 | tf_op jit(solution)/shard_map/ppermute | solution.py:464
  215.7 20.8 %collective-permute-start.7 = (bf16[192,2304]{1,0:T(8,128)(2,1)S(1)}, bf16[192,2304]{1,0:T(8,128)(2,1)S(1)}, u32[]{:S(2)}, u32[]{:S(2)}) collective-permute-start(bf16[192,2304]{1,0:T(8,128)(2,1)S(1)} %bitcast.23), channel_id=1, source_target_pairs={{0,4},{4,8},{8,12},{12,0},{1,5},{5,9},{9,13},{13,1},{2,6},{6,10},{... | collective-permute-start | bytes 2654216 | tf_op jit(solution)/shard_map/ppermute | solution.py:463
  234.6 9.4 %copy-start.1 = (bf16[192,2304]{1,0:T(8,128)(2,1)}, bf16[192,2304]{1,0:T(8,128)(2,1)S(1)}, u32[]{:S(2)}) copy-start(bf16[192,2304]{1,0:T(8,128)(2,1)S(1)} %collective-permute-done.8.above) | copy-start | bytes 2654212
  234.6 9.3 %collective-permute-start.10 = (bf16[96,2304]{1,0:T(8,128)(2,1)S(1)}, bf16[96,2304]{1,0:T(8,128)(2,1)S(1)}, u32[]{:S(2)}, u32[]{:S(2)}) collective-permute-start(bf16[96,2304]{1,0:T(8,128)(2,1)S(1)} %slice.90), channel_id=1, source_target_pairs={{0,12},{4,0},{8,4},{12,8},{1,13},{5,1},{9,5},{13,9},{2,14},{6,2},{... | collective-permute-start | bytes 1327112 | tf_op jit(solution)/shard_map/ppermute | solution.py:466
  236.6 7.4 %copy-start.2 = (bf16[192,2304]{1,0:T(8,128)(2,1)}, bf16[192,2304]{1,0:T(8,128)(2,1)S(1)}, u32[]{:S(2)}) copy-start(bf16[192,2304]{1,0:T(8,128)(2,1)S(1)} %collective-permute-done.7.below) | copy-start | bytes 2654212
  236.6 10.1 %collective-permute-start.9 = (bf16[96,2304]{1,0:T(8,128)(2,1)S(1)}, bf16[96,2304]{1,0:T(8,128)(2,1)S(1)}, u32[]{:S(2)}, u32[]{:S(2)}) collective-permute-start(bf16[96,2304]{1,0:T(8,128)(2,1)S(1)} %slice.89), channel_id=1, source_target_pairs={{0,4},{4,8},{8,12},{12,0},{1,5},{5,9},{9,13},{13,1},{2,6},{6,10},{... | collective-permute-start | bytes 1327112 | tf_op jit(solution)/shard_map/ppermute | solution.py:465
  244.0 2.8 %copy-start.11 = (bf16[96,2304]{1,0:T(8,128)(2,1)}, bf16[96,2304]{1,0:T(8,128)(2,1)S(1)}, u32[]{:S(2)}) copy-start(bf16[96,2304]{1,0:T(8,128)(2,1)S(1)} %collective-permute-done.10.far_b) | copy-start | bytes 1327108
  246.7 0.8 copy-start.12

commit v2 on v1

v2 whole, which is shorter than its diff:
```python
import functools

import jax
import jax.numpy as jnp
from jax import lax
from jax.experimental import pallas as pl
from jax.experimental.pallas import tpu as pltpu
from jax.sharding import Mesh
from jax.sharding import PartitionSpec as P

B = 64
KA = 8
KP = 4
A3G = 12
BR = 40
CR = 10
FR = BR * B
BAND = CR * B
L3 = A3G * B
Q_ROWS = 3 * B
NUM_ROWS = 16
AGG_AT = BR * KP
RELAYS = (13, 11)
BF = jnp.bfloat16
F32 = jnp.float32
SMEM = pl.BlockSpec(memory_space=pltpu.SMEM)
VMEM = pl.BlockSpec(memory_space=pltpu.VMEM)
ANY = pl.BlockSpec(memory_space=pl.ANY)
ROW = ("z", "x")
ALL = ("grp", "z", "x")


def kernel_params():
    return pltpu.CompilerParams(vmem_limit_bytes=56 << 20)


def cost(gflop, mbytes):
    return pl.CostEstimate(flops=gflop * 10**9, bytes_accessed=mbytes * 10**6, transcendentals=0)


def rows64(i):
    return pl.ds(pl.multiple_of(i * B, B), B)


def rows_at(start, height):
    return pl.ds(pl.multiple_of(start, height), height)


def half_of(shape):
    return lax.broadcasted_iota(jnp.int32, shape, 1) // B


def pta_kernel(cols, count, pcol, a_ref, p_ref, out_ref, acc):
    step = pl.program_id(0)
    pairs = acc.shape[0]
    height = out_ref.shape[0]
    some = height // B

    @pl.when(step == 0)
    def start():
        def clear(j, c):
            for q in range(pairs):
                acc[q, rows_at(j * 128, 128), :] = jnp.zeros((128, 128), F32)
            return c

        lax.fori_loop(0, 3 * BR // 2, clear, 0)

    @pl.when(step < BR // some)
    def accumulate():
        half = half_of((B, 2 * B))
        slot = lax.broadcasted_iota(jnp.int32, (KA * B, B), 0) // B

        def row(n, c):
            i = step * some + n
            r = rows64(i)
            at = a_ref[r, :].T
            at = jnp.where(slot < count[i], at, jnp.zeros_like(at))
            parts = []
            for m in range(KP):
                t = pcol[KP * i + m]
                x = p_ref[r, (m // 2) * 128 : (m // 2) * 128 + 128]
                y = jnp.concatenate([x[:, B:], x[:, :B]], axis=1)
                x = jnp.where(t % 2 == m % 2, x, y)
                parts.append(jnp.where(half == t % 2, x, jnp.zeros_like(x)))
            rhs = jnp.concatenate(parts, axis=1)
            for k in range(KA):
                z = jnp.dot(at[k * B : k * B + B, :], rhs, preferred_element_type=F32)
                rr = rows64(cols[i, k])
                for m in range(KP):
                    acc[pcol[KP * i + m] // 2, rr, :] += z[:, m * 128 : m * 128 + 128]
            return c

        lax.fori_loop(0, some, row, 0, unroll=2)

    base = step * height

    def finish(j, c):
        src = rows_at(base + j * 64, 64)
        dst = rows64(j)
        for q in range(pairs):
            out_ref[dst, q * 128 : q * 128 + 128] = acc[q, src, :].astype(BF)
        return c

    lax.fori_loop(0, height // 64, finish, 0)


def pta(cols, count, pcol, a, p):
    steps = 12
    height = 3 * FR // steps
    return pl.pallas_call(
        pta_kernel,
        grid=(steps,),
        out_shape=jax.ShapeDtypeStruct((3 * FR, 2 * BAND), BF),
        in_specs=[SMEM, SMEM, SMEM, VMEM, VMEM],
        out_specs=pl.BlockSpec((height, 2 * BAND), lambda s: (s, 0)),
        scratch_shapes=[pltpu.VMEM((CR, 3 * FR, 128), F32)],
        compiler_params=kernel_params(),
        cost_estimate=cost(12, 24),
        name="pta",
    )(cols, count, pcol, a, p)


def build_pt(wcol, p_ref, pt):
    def clear(j, c):
        pt[rows64(j), :] = jnp.zeros((B, FR), BF)
        return c

    lax.fori_loop(0, 2 * CR, clear, 0)
    half = half_of((B, 2 * B))

    def pair(jp, c):
        lanes = pl.ds(pl.multiple_of(jp * 128, 128), 128)
        xt = p_ref[lanes, :].T
        for n in range(KP):
            x = xt[n * B : n * B + B, :]
            for s in range(2):
                r = rows64(wcol[KP * (2 * jp + s) + n])
                pt[r, lanes] = jnp.where(half == s, x, pt[r, lanes])
        return c

    lax.fori_loop(0, BR // 2, pair, 0)


def tiles(height, body):
    def tile(i, c):
        body(rows_at(i * 320, 320))
        return c

    lax.fori_loop(0, height // 320, tile, 0)


def shifted(r, by):
    return pl.ds(pl.multiple_of(r.start + by, 320), r.size)


def halo_kernel(part, wcol, p_hbm, pat_hbm, low, up, rest_low, rest_up, pt, pat, p_ref, sems):
    copies = [
        pltpu.make_async_copy(p_hbm.at[pl.ds(0, FR), :], p_ref, sems.at[0]),
        pltpu.make_async_copy(pat_hbm.at[pl.ds(part * FR, FR), :], pat, sems.at[1]),
    ]
    for copy in copies:
        copy.start()
    copies[0].wait()
    build_pt(wcol, p_ref, pt)
    copies[1].wait()
    final, open_from = (0, BAND) if part == 0 else (BAND, 0)

    def alone(r):
        z = jnp.dot(pt[shifted(r, final), :], pat[...], preferred_element_type=F32).astype(BF)
        low[r, :] = z[:, :BAND]
        up[r, :] = z[:, BAND:]

    def shared(r):
        z = jnp.dot(pt[shifted(r, open_from), :], pat[...], preferred_element_type=F32)
        rest_low[r, :] = z[:, :BAND]
        rest_up[r, :] = z[:, BAND:]

    tiles(BAND, alone)
    tiles(BAND, shared)


def halo_product(part, wcol, p, pat):
    return pl.pallas_call(
        functools.partial(halo_kernel, part),
        out_shape=[jax.ShapeDtypeStruct((BAND, BAND), t) for t in (BF, BF, F32, F32)],
        in_specs=[SMEM, ANY, ANY],
        out_specs=[VMEM] * 4,
        scratch_shapes=[
            pltpu.VMEM((2 * BAND, FR), BF),
            pltpu.VMEM((FR, 2 * BAND), BF),
            pltpu.VMEM((FR, KP * B), BF),
            pltpu.SemaphoreType.DMA((2,)),
        ],
        compiler_params=kernel_params(),
        cost_estimate=cost(8, 14),
        name=f"halo_product{part}",
    )(wcol, p, pat)


def own_kernel(which, wcol, p_ref, pat_hbm, rest0, rest2, out_ref, pt, pat, sem):
    mine = pat_hbm.at[pl.ds(FR, FR), pl.ds(which * BAND, BAND)]
    copy = pltpu.make_async_copy(mine, pat, sem)
    copy.start()
    build_pt(wcol, p_ref, pt)
    copy.wait()
    for rest, start in ((rest0, 0), (rest2, BAND)):
        def body(r):
            here = shifted(r, start)
            z = rest[r, :] + jnp.dot(pt[here, :], pat[...], preferred_element_type=F32)
            out_ref[here, :] = z.astype(BF)

        tiles(BAND, body)


def own_product(which, wcol, p, pat, rest0, rest2):
    return pl.pallas_call(
        functools.partial(own_kernel, which),
        out_shape=jax.ShapeDtypeStruct((2 * BAND, BAND), BF),
        in_specs=[SMEM, VMEM, ANY, VMEM, VMEM],
        out_specs=VMEM,
        scratch_shapes=[
            pltpu.VMEM((2 * BAND, FR), BF),
            pltpu.VMEM((FR, BAND), BF),
            pltpu.SemaphoreType.DMA,
        ],
        compiler_params=kernel_params(),
        cost_estimate=cost(1, 1),
        name=f"own_product{which}",
    )(wcol, p, pat, rest0, rest2)


def level3_kernel(mine, flags, agg0, agg1, agg2, agg3, q0, q1, q2, q3, outer0, inner, outer3, *refs):
    outs, (qt, u, q, sems) = refs[:2], refs[2:]
    copies = []
    for s, ref in enumerate((q0, q1, q2, q3)):
        start = ref.shape[0] - Q_ROWS - NUM_ROWS
        copies.append(pltpu.make_async_copy(ref.at[pl.ds(start, Q_ROWS), :], q.at[s], sems.at[s]))
        copies[-1].start()
    half = half_of((B, 2 * B))
    qt[...] = jnp.zeros_like(qt)
    u[...] = jnp.zeros_like(u)
    for s, agg in enumerate((agg0, agg1, agg2, agg3)):
        copies[s].wait()
        for cp in range(CR // 2):
            x = q[s, cp // 2 * B : cp // 2 * B + B, cp % 2 * 128 : cp % 2 * 128 + 128]
            for e in range(2):
                r = rows64(agg[AGG_AT + 2 * cp + e])
                lanes = slice(cp * 128, cp * 128 + 128)
                qt[s, r, lanes] = jnp.where(half == e, x, qt[s, r, lanes])
    def expand(s, here):
        u[flags[s]] += jnp.dot(qt[s], here, preferred_element_type=F32)

    def middle(s, c):
        expand(s + 1, inner[rows_at(s * BAND, BAND), :])
        return c

    expand(0, outer0[...])
    lax.fori_loop(0, 2, middle, 0)
    expand(3, outer3[...])

    def finish(to):
        z = lax.dot_general(
            u[to].astype(BF), qt[mine], (((1,), (1,)), ((), ())), preferred_element_type=F32
        )
        outs[to][...] = z.T.astype(BF)

    finish(0)
    pl.when(flags[4] == 1)(lambda: finish(1))

    @pl.when(flags[4] == 0)
    def empty():
        outs[1][...] = jnp.zeros((L3, L3), BF)


def level3_parts(mine, flags, aggs, qs, parts):
    return pl.pallas_call(
        functools.partial(level3_kernel, mine),
        out_shape=[jax.ShapeDtypeStruct((L3, L3), BF)] * 2,
        in_specs=[SMEM] * 5 + [ANY] * 4 + [VMEM] * 3,
        out_specs=[VMEM] * 2,
        scratch_shapes=[
            pltpu.VMEM((4, L3, BAND), BF),
            pltpu.VMEM((2, L3, BAND), F32),
            pltpu.VMEM((4, Q_ROWS, KP * B), BF),
            pltpu.SemaphoreType.DMA((4,)),
        ],
        compiler_params=kernel_params(),
        cost_estimate=cost(1, 1),
        name=f"level3_parts{mine}",
    )(flags, *aggs, *qs, *parts)


def level2_kernel(low_l, low_m, low_h, got_l, got_m, got_h, out_ref):
    s = pl.program_id(0)

    def pick(k, left, middle, right):
        return jnp.where(k == 0, left[...], jnp.where(k == 3, right[...], middle[...])).T.astype(F32)

    mine = jnp.where(s >= 1, pick(s - 1, low_l, low_m, low_h), 0.0)
    theirs = jnp.where(s <= 3, pick(s, got_l, got_m, got_h), 0.0)
    out_ref[...] = (mine + theirs).astype(BF)


def level2_rows(low, got):
    one = pl.BlockSpec((BAND, BAND), lambda s: (0, 0))
    return pl.pallas_call(
        level2_kernel,
        grid=(5,),
        out_shape=jax.ShapeDtypeStruct((BAND, 5 * BAND), BF),
        in_specs=[
            one,
            pl.BlockSpec((BAND, BAND), lambda s: (jnp.clip(s - 2, 0, 1), 0)),
            one,
            one,
            pl.BlockSpec((BAND, BAND), lambda s: (jnp.clip(s - 1, 0, 1), 0)),
            one,
        ],
        out_specs=pl.BlockSpec((BAND, BAND), lambda s: (0, s)),
        compiler_params=kernel_params(),
        cost_estimate=cost(1, 14),
        name="level2_rows",
    )(*low, *got)


def place_kernel(z, own, below, above, out_ref):
    g = pl.program_id(0)

    @pl.when(g == 0)
    def here():
        out_ref[...] = own[...].astype(F32)

    @pl.when(g == 1)
    def following():
        out_ref[...] = above[...].astype(F32)

    @pl.when(g == 2)
    def previous():
        out_ref[...] = below[...].astype(F32)


def place_far_kernel(z, half_a, half_b, placed, out_ref):
    cut = half_a.shape[0]
    out_ref[:cut, :] = half_a[...].astype(F32)
    out_ref[cut:, :] = half_b[...].astype(F32)


def place(z, own, below, above):
    height, width = own.shape
    return pl.pallas_call(
        place_kernel,
        grid_spec=pltpu.PrefetchScalarGridSpec(
            num_scalar_prefetch=1,
            grid=(3,),
            in_specs=[VMEM] * 3,
            out_specs=pl.BlockSpec((height, width), lambda g, z: ((z[0] + jnp.where(g == 2, 3, g)) % 4, 0)),
        ),
        out_shape=jax.ShapeDtypeStruct((4 * height, width), F32),
        compiler_params=kernel_params(),
        cost_estimate=cost(1, 8),
        name="place",
    )(z, own, below, above)


def place_far(z, half_a, half_b, placed):
    height, width = placed.shape[0] // 4, placed.shape[1]
    return pl.pallas_call(
        place_far_kernel,
        grid_spec=pltpu.PrefetchScalarGridSpec(
            num_scalar_prefetch=1,
            grid=(1,),
            in_specs=[VMEM, VMEM, ANY],
            out_specs=pl.BlockSpec((height, width), lambda g, z: ((z[0] + 2) % 4, 0)),
        ),
        out_shape=jax.ShapeDtypeStruct(placed.shape, F32),
        input_output_aliases={3: 0},
        compiler_params=kernel_params(),
        cost_estimate=cost(1, 3),
        name="place_far",
    )(z, half_a, half_b, placed)


def moved(array, by):
    devices = lax.axis_size(ALL)
    pairs = [(i, i + by) for i in range(devices) if 0 <= i + by < devices]
    return lax.ppermute(array, ALL, pairs)


def per_device(a_blocks, a_cols, a_count, p_blocks, p_cols, q2_blocks, agg3):
    row_size = lax.axis_size(ROW)
    sz, sx = lax.axis_size("z"), lax.axis_size("x")
    groups = lax.axis_size("grp")
    device = lax.axis_index(ALL)
    row = lax.axis_index(ROW)
    width = KP * B
    cols = a_cols - (device - 1) * BR
    wcol = (p_cols - device * CR).reshape(-1)
    numbers = jnp.concatenate([wcol, agg3 % A3G, jnp.zeros((width - BR * KP - CR,), jnp.int32)])

    tail = jnp.transpose(q2_blocks.reshape(CR, B, B), (2, 0, 1)).reshape(B, BAND)
    tail = jnp.pad(tail, ((0, 0), (0, 3 * width - BAND))).reshape(B, 3, width)
    tail = jnp.transpose(tail, (1, 0, 2)).reshape(Q_ROWS, width)
    small = jnp.pad(numbers.astype(BF)[None], ((0, NUM_ROWS - 1), (0, 0)))
    tail = jnp.concatenate([tail, small], axis=0)
    mine = jnp.concatenate([p_blocks, tail], axis=0)
    lower = moved(mine, 1)
    higher = moved(mine, -1)

    def numbers_of(array):
        return array[array.shape[0] - NUM_ROWS].astype(jnp.int32)

    pat = pta(cols, a_count, numbers, a_blocks, p_blocks)
    far = moved(tail, -2)
    pat, far = lax.optimization_barrier((pat, far))
    nlow, nhigh, nfar = numbers_of(lower), numbers_of(higher), numbers_of(far)
    aggs = (nlow, numbers, nhigh, nfar)

    low_h, up_h, rest2_low, rest2_up = halo_product(2, nhigh, higher, pat)
    got_h = moved(up_h, 1)
    low_l, up_l, rest0_low, rest0_up = halo_product(0, nlow, lower, pat)
    got_l = moved(up_l, 1)
    rest0_up, got_h = lax.optimization_barrier((rest0_up, got_h))
    up_m = own_product(1, numbers, p_blocks, pat, rest0_up, rest2_up)
    got_m = moved(up_m, 1)
    rest0_low, up_m = lax.optimization_barrier((rest0_low, up_m))
    low_m = own_product(0, numbers, p_blocks, pat, rest0_low, rest2_low)
    low_m, got_l = lax.optimization_barrier((low_m, got_l))

    qs = (lower, tail, higher, far)
    first, last = row == 0, row == row_size - 1
    ahead = row + 2 >= row_size
    flags = jnp.stack([first, row < 0, last, ahead, first | ahead]).astype(jnp.int32)
    nfar, low_m = lax.optimization_barrier((nfar, low_m))
    aggs = (nlow, numbers, nhigh, nfar)
    upper_c, upper_s = level3_parts(2, flags, aggs, qs, (up_l, up_m, up_h))

    def over(to):
        return [(g * row_size + row_size - 1, (g + 1) * row_size + to(g)) for g in range(groups - 1)]

    late_s = lax.ppermute(upper_c, ALL, over(lambda g: RELAYS[0] if g % 2 else RELAYS[1]))
    late_c = lax.ppermute(upper_s, ALL, over(lambda g: row_size - 1))
    low_l, upper_c = lax.optimization_barrier((low_l, upper_c))
    lower_c, lower_s = level3_parts(1, flags, aggs, qs, (low_l, low_m, low_h))
    lower_c, got_m = lax.optimization_barrier((lower_c, got_m))

    def total(lower_part, upper_part, late):
        upper_part = jnp.where(last, 0.0, upper_part.astype(F32))
        return (lower_part.astype(F32) + upper_part + late.astype(F32)).astype(BF)

    main = jnp.concatenate([total(lower_c, upper_c, late_c), total(lower_s, upper_s, late_s)], axis=1)

    chunk = L3 // row_size
    part = lax.all_to_all(main, ROW, 0, 0, tiled=True).reshape(row_size, chunk, 2 * L3)
    left = part[0, :, L3:].astype(F32) + sum(part[r, :, L3:].astype(F32) for r in RELAYS)
    right = part[row_size - 2, :, L3:].astype(F32) + part[row_size - 1, :, L3:].astype(F32)
    middle = jnp.sum(part[:, :, :L3].astype(F32), axis=0)
    whole = jnp.concatenate([left, middle, right], axis=1).astype(BF)

    whole = lax.all_to_all(jnp.tile(whole, (sx, 1)), "x", 0, 0, tiled=True)
    tall = L3 // sz
    onward = [(i, (i + 1) % sz) for i in range(sz)]
    back = [(i, (i - 1) % sz) for i in range(sz)]
    below = lax.ppermute(whole, "z", onward)
    above = lax.ppermute(whole, "z", back)
    level2 = level2_rows((low_l, low_m, low_h), (got_l, got_m, got_h))
    below, above, level2 = lax.optimization_barrier((below, above, level2))
    far_a = lax.ppermute(below[: tall // 2], "z", onward)
    far_b = lax.ppermute(above[tall // 2 :], "z", back)
    z = lax.axis_index("z").astype(jnp.int32)[None]
    level3 = place_far(z, far_a, far_b, place(z, whole, below, above))
    return (level2, level3)


def solution(mesh):
    grp, row = mesh.devices.shape
    fine = Mesh(mesh.devices.reshape(grp, 4, row // 4), ALL)
    in_specs = (P(ALL, None), P(ALL, None), P(ALL), P(ALL, None), P(ALL, None), P(ALL, None), P(ALL))
    out_specs = (P(ALL, None), P("grp", None))
    return jax.shard_map(
        per_device, mesh=fine, in_specs=in_specs, out_specs=out_specs, check_vma=False
    )
```

time: 253 us -> 238 us (0.941); the launches traced: 253 us -> 235 us
  Pallas kernels: 126 us -> 118 us
  blocking collectives: 55.9 us -> 51.7 us
  local copies, waits for them, and re-layouts: 9.24 us -> 5.46 us
  waiting for transfers between devices: 20.5 us -> 17.6 us
    ppermute x1, waiting for transfers between devices: 17.7 us -> 0.11 us  [per_device(): above = lax.ppermute(whole, 'z', back)]
    ppermute x1, waiting for transfers between devices: 0.01 us -> 9.24 us  [per_device(): below = lax.ppermute(whole, 'z', onward)]
    pallas_call x4 -> x5, Pallas kernels: 63.6 us -> 55.8 us  [the longest x2 29.5 us: halo_product(): pl.pallas_call(functools.partial(halo_kernel, part), out_shape=[jax.Shape...]
    ppermute x5 -> x6, waiting for transfers between devices: 0.01 us -> 6.44 us  [moved(): return lax.ppermute(array, ALL, pairs)]
    all_to_all x1, blocking collectives: 40.8 us -> 37.5 us  [per_device(): lax.all_to_all(main, ROW, 0, 0, tiled=True).reshape(row_size, chunk, 2 * L3)]
    ppermute x5 -> x6, starting transfers between devices: 21.9 us -> 22.7 us  [moved(): return lax.ppermute(array, ALL, pairs)]
  transfers between devices with their start and end apart: 11 -> 12, of which waited for: 2 -> 6; matrix products, arithmetic and copies ran while one was open for 5% -> 3% of each run, Pallas kernels for 48% -> 49%
where the time goes in v2:
time: 238 us; the launch traced here: 235 us
  Pallas kernels  118 us (50%)
  blocking collectives  51.7 us (22%)
  starting transfers between devices  30.8 us (13%)
  waiting for transfers between devices  17.6 us (7%)
  other arithmetic  10.4 us (4%)
  local copies, waits for them, and re-layouts  5.46 us (2%)
    all_to_all x1, blocking collectives, per_device(): lax.all_to_all(main, ROW, 0, 0, tiled=True).reshape(row_size, chunk, 2 * L3)  37.5 us
    pallas_call x2, Pallas kernels, halo_product(): pl.pallas_call(functools.partial(halo_kernel, part), out_shape=[jax.Shape...  29.5 us
    pallas_call x1, Pallas kernels, pta(): pl.pallas_call(pta_kernel, grid=(steps,), out_shape=jax.ShapeDtypeStruct(...  27.3 us
    pallas_call x2, Pallas kernels, own_product(): pl.pallas_call(functools.partial(own_kernel, which), out_shape=jax.ShapeD...  23.7 us
    pallas_call x2, Pallas kernels, level3_parts(): pl.pallas_call(functools.partial(level3_kernel, mine), out_shape=[jax.Sha...  23.5 us
    ppermute x6, starting transfers between devices, moved(): return lax.ppermute(array, ALL, pairs)  22.7 us
    all_to_all x1, blocking collectives, per_device(): whole = lax.all_to_all(jnp.tile(whole, (sx, 1)), 'x', 0, 0, tiled=True)  14.2 us
    ppermute x1, waiting for transfers between devices, per_device(): below = lax.ppermute(whole, 'z', onward)  9.24 us
  transfers between devices with their start and end apart: 12, of which 6 were waited for; matrix products, arithmetic and copies ran while one was open for 3% of the time, Pallas kernels for 49%

profile of v2, /device:TPU:8, one launch (start us, length us, event | category | flops | bytes accessed | tf_op | source)
XLA Modules:
  0.0 235.1 jit_solution(5434783978306024504)
XLA Ops:
  2.4 1.1 reshape.112
  3.7 2.5 %pad_maximum_fusion.1 = bf16[2768,256]{1,0:T(8,128)(2,1)} fusion(bf16[16,256]{1,0:T(8,128)(2,1)S(1)} %pad.9, bf16[192,256]{1,0:T(8,128)(2,1)S(1)} %bitcast.27, bf16[2560,256]{1,0:T(8,128)(2,1)} %p_ref.5), kind=kLoop, calls=%fused_computation.3 | loop fusion | flops 4251648 | bytes 2834432 | tf_op jit(solution)/shard_map/concatenate | solution.py:404
  6.3 7.5 %collective-permute-start.1 = (bf16[2768,256]{1,0:T(8,128)(2,1)}, bf16[2768,256]{1,0:T(8,128)(2,1)S(1)}, u32[]{:S(2)}, u32[]{:S(2)}) collective-permute-start(bf16[2768,256]{1,0:T(8,128)(2,1)} %pad_maximum_fusion.1), channel_id=1, source_target_pairs={{1,0},{2,1},{3,2},{4,3},{5,4},{6,5},{7,6},{8,7},{9,8},{10,9},{11,1... | collective-permute-start | bytes 4251656 | tf_op jit(solution)/shard_map/ppermute | solution.py:385
  13.7 1.9 collective-permute-start
  15.7 3.6 %collective-permute-start.2 = (bf16[208,256]{1,0:T(8,128)(2,1)S(1)}, bf16[208,256]{1,0:T(8,128)(2,1)S(1)}, u32[]{:S(2)}, u32[]{:S(2)}) collective-permute-start(bf16[208,256]{1,0:T(8,128)(2,1)S(1)} %pad_maximum_fusion.3.q1), channel_id=1, source_target_pairs={{2,0},{3,1},{4,2},{5,3},{6,4},{7,5},{8,6},{9,7},{10,8},{11,9},{12,... | collective-permute-start | bytes 319496 | tf_op jit(solution)/shard_map/ppermute | solution.py:385
  20.9 27.3 %pta.1.pat_hbm = bf16[7680,1280]{1,0:T(8,128)(2,1)} custom-call(s32[40,8]{1,0:T(8,128)} %broadcast_subtract_fusion.cols, s32[40]{0:T(128)} %count.1, s32[256]{0:T(256)} %pad_add_fusion.pcol.wcol.agg1, bf16[2560,512]{1,0:T(8,128)(2,1)} %a_ref.1, bf16[2560,256]{1,0:T(8,128)(2,1)} %p_ref.5), custom_call_target="tpu_custom_call" | custom-call | flops 12000000000 | bytes 24000000 | tf_op jit(solution)/shard_map/pta/pallas_call | solution.py:110
  48.2 1.3 collective-permute-done.2.q3
  50.7 14.8 %halo_product2.1 = (bf16[640,640]{1,0:T(8,128)(2,1)}, bf16[640,640]{1,0:T(8,128)(2,1)}, f32[640,640]{1,0:T(8,128)}, f32[640,640]{1,0:T(8,128)}) custom-call(s32[256]{0:T(256)} %bitcast.32, bf16[2768,256]{1,0:T(8,128)(2,1)} %copy-done, bf16[7680,1280]{1,0:T(8,128)(2,1)} %pta.1.pat_hbm), custom_call_target="tpu_custom_call" | custom-call | flops 8000000000 | bytes 14000000 | tf_op jit(solution)/shard_map/halo_product2/pallas_call | solution.py:183
  65.5 5.7 %collective-permute-start.3 = (bf16[640,640]{1,0:T(8,128)(2,1)}, bf16[640,640]{1,0:T(8,128)(2,1)S(1)}, u32[]{:S(2)}, u32[]{:S(2)}) collective-permute-start(bf16[640,640]{1,0:T(8,128)(2,1)} %get-tuple-element.35.outer3), channel_id=1, source_target_pairs={{0,1},{1,2},{2,3},{3,4},{4,5},{5,6},{6,7},{7,8},{8,9},{9,10},{10,1... | collective-permute-start | bytes 2457608 | tf_op jit(solution)/shard_map/ppermute | solution.py:385
  72.3 14.8 %halo_product0.1 = (bf16[640,640]{1,0:T(8,128)(2,1)}, bf16[640,640]{1,0:T(8,128)(2,1)}, f32[640,640]{1,0:T(8,128)}, f32[640,640]{1,0:T(8,128)}) custom-call(s32[256]{0:T(256)} %bitcast.35, bf16[2768,256]{1,0:T(8,128)(2,1)} %copy-done.1, bf16[7680,1280]{1,0:T(8,128)(2,1)} %pta.1.pat_hbm), custom_call_target="tpu_custom_call" | custom-call | flops 8000000000 | bytes 14000000 | tf_op jit(solution)/shard_map/halo_product0/pallas_call | solution.py:183
  87.0 1.9 collective-permute-start.4
  90.2 1.7 collective-permute-done.3.got_h
  92.0 12.0 %own_product1.1.inner = bf16[1280,640]{1,0:T(8,128)(2,1)} custom-call(s32[256]{0:T(256)} %pad_add_fusion.pcol.wcol.agg1, bf16[2560,256]{1,0:T(8,128)(2,1)} %p_ref.5, bf16[7680,1280]{1,0:T(8,128)(2,1)} %pta.1.pat_hbm, f32[640,640]{1,0:T(8,128)} %get-tuple-element.36.rest0, f32[640,640]{1,0:T(8,128)} %get-tuple-element.37.rest2), custom_call_target="tpu_custom_call" | custom-call | flops 1000000000 | bytes 1000000 | tf_op jit(solution)/shard_map/own_product1/pallas_call | solution.py:216
  104.0 2.1 collective-permute-start.5
  106.1 11.7 %own_product0.1.inner.low_m = bf16[1280,640]{1,0:T(8,128)(2,1)} custom-call(s32[256]{0:T(256)} %pad_add_fusion.pcol.wcol.agg1, bf16[2560,256]{1,0:T(8,128)(2,1)} %p_ref.5, bf16[7680,1280]{1,0:T(8,128)(2,1)} %pta.1.pat_hbm, f32[640,640]{1,0:T(8,128)} %get-tuple-element.38.rest0, f32[640,640]{1,0:T(8,128)} %get-tuple-element.39.rest2), custom_call_target="tpu_custom_call" | custom-call | flops 1000000000 | bytes 1000000 | tf_op jit(solution)/shard_map/own_product0/pallas_call | solution.py:216
  117.9 11.8 %level3_parts2.1 = (bf16[768,768]{1,0:T(8,128)(2,1)}, bf16[768,768]{1,0:T(8,128)(2,1)}) custom-call(s32[5]{0:T(128)} %convert_element_type.93.flags, s32[256]{0:T(256)} %bitcast.36, s32[256]{0:T(256)} %pad_add_fusion.pcol.wcol.agg1, s32[256]{0:T(256)} %bitcast.33, s32[256]{0:T(256)} %bitcast.38, bf16[2768,256]{1,0:T(8,128)(2,1)} %copy-done.1, ...), custom_call_target="tpu_custom_call" | custom-call | flops 1000000000 | bytes 1000000 | tf_op jit(solution)/shard_map/level3_parts2/pallas_call | solution.py:276
  129.6 0.7 collective-permute-start.7
  130.4 0.7 collective-permute-start.6
  131.1 11.8 %level3_parts1.1 = (bf16[768,768]{1,0:T(8,128)(2,1)}, bf16[768,768]{1,0:T(8,128)(2,1)}) custom-call(s32[5]{0:T(128)} %convert_element_type.93.flags, s32[256]{0:T(256)} %bitcast.37, s32[256]{0:T(256)} %pad_add_fusion.pcol.wcol.agg1, s32[256]{0:T(256)} %bitcast.34, s32[256]{0:T(256)} %bitcast.39, bf16[2768,256]{1,0:T(8,128)(2,1)} %copy-done.1, ...), custom_call_target="tpu_custom_call" | custom-call | flops 1000000000 | bytes 1000000 | tf_op jit(solution)/shard_map/level3_parts1/pallas_call | solution.py:276
  143.0 1.9 add_convert_fusion
  144.9 3.4 %collective-permute-done.5.got_m = bf16[1280,640]{1,0:T(8,128)(2,1)S(1)} collective-permute-done((bf16[1280,640]{1,0:T(8,128)(2,1)}, bf16[1280,640]{1,0:T(8,128)(2,1)S(1)}, u32[]{:S(2)}, u32[]{:S(2)}) %collective-permute-start.5) | collective-permute-done | bytes 1638432 | tf_op jit(solution)/shard_map/ppermute | solution.py:385
  149.7 37.5 %all_to_all.17 = bf16[16,48,1536]{2,1,0:T(8,128)(2,1)S(1)} all-to-all(bf16[16,48,1536]{2,1,0:T(8,128)(2,1)S(1)} %bitcast.23), channel_id=1, replica_groups=mesh['grp'=8,'z'=4,'x'=4] {'z','x'}, dimensions={0} | all-to-all | bytes 4718592 | tf_op jit(solution)/shard_map/all_to_all | solution.py:452
  187.4 14.2 %all_to_all.18 = bf16[4,48,2304]{2,1,0:T(8,128)(2,1)S(1)} all-to-all(bf16[4,48,2304]{2,1,0:T(8,128)(2,1)S(1)} %tile.2), channel_id=1, replica_groups=mesh['grp'=8,'z'=4,'x'=4] {'x'}, dimensions={0} | all-to-all | bytes 1769472 | tf_op jit(solution)/shard_map/all_to_all | solution.py:458
  202.1 2.7 %collective-permute-start.9 = (bf16[192,2304]{1,0:T(8,128)(2,1)S(1)}, bf16[192,2304]{1,0:T(8,128)(2,1)S(1)}, u32[]{:S(2)}, u32[]{:S(2)}) collective-permute-start(bf16[192,2304]{1,0:T(8,128)(2,1)S(1)} %bitcast.25), channel_id=1, source_target_pairs={{0,12},{4,0},{8,4},{12,8},{1,13},{5,1},{9,5},{13,9},{2,14},{6,2},{... | collective-permute-start | bytes 2654216 | tf_op jit(solution)/shard_map/ppermute | solution.py:463
  204.9 7.2 %level2_rows.1 = bf16[640,3200]{1,0:T(8,128)(2,1)} custom-call(bf16[640,640]{1,0:T(8,128)(2,1)} %get-tuple-element.46.outer0.low_l, bf16[1280,640]{1,0:T(8,128)(2,1)} %own_product0.1.inner.low_m, bf16[640,640]{1,0:T(8,128)(2,1)} %get-tuple-element.48.outer3.low_h, bf16[640,640]{1,0:T(8,128)(2,1)} %copy-done.11, bf16[1280,640]{1,0:T(8,128)(2,1)} %copy-done.5, ...), custom_call_target="tpu_custom_call" | custom-call | flops 1000000000 | bytes 14000000 | tf_op jit(solution)/shard_map/level2_rows/pallas_call | solution.py:306
  212.1 9.2 %collective-permute-done.8.below = bf16[192,2304]{1,0:T(8,128)(2,1)S(1)} collective-permute-done((bf16[192,2304]{1,0:T(8,128)(2,1)S(1)}, bf16[192,2304]{1,0:T(8,128)(2,1)S(1)}, u32[]{:S(2)}, u32[]{:S(2)}) %collective-permute-start.8) | collective-permute-done | bytes 884768 | tf_op jit(solution)/shard_map/ppermute | solution.py:462
  222.0 2.9 %collective-permute-start.11 = (bf16[96,2304]{1,0:T(8,128)(2,1)S(1)}, bf16[96,2304]{1,0:T(8,128)(2,1)S(1)}, u32[]{:S(2)}, u32[]{:S(2)}) collective-permute-start(bf16[96,2304]{1,0:T(8,128)(2,1)S(1)} %slice.43), channel_id=1, source_target_pairs={{0,12},{4,0},{8,4},{12,8},{1,13},{5,1},{9,5},{13,9},{2,14},{6,2},{... | collective-permute-start | bytes 1327112 | tf_op jit(solution)/shard_map/ppermute | solution.py:467
  224.9 4.4 %place.1.placed = f32[768,2304]{1,0:T(8,128)} custom-call(s32[1]{0:T(128)} %bitcast.18.z, bf16[192,2304]{1,0:T(8,128)(2,1)} %bitcast.26, bf16[192,2304]{1,0:T(8,128)(2,1)} %copy-done.3, bf16[192,2304]{1,0:T(8,128)(2,1)} %copy-done.4), custom_call_target="tpu_custom_call" | custom-call | flops 1000000000 | bytes 8000000 | tf_op jit(solution)/shard_map/place/pallas_call | solution.py:349
  229.3 1.8 collective-permute-done.10.half_a
  231.1 0.8 copy-done.12
  231.9 0.8 copy-done.13
  232.6 2.5 %place_far.1 = f32[768,2304]{1,0:T(8,128)} custom-call(s32[1]{0:T(128)} %bitcast.18.z, bf16[96,2304]{1,0:T(8,128)(2,1)} %copy-done.12, bf16[96,2304]{1,0:T(8,128)(2,1)} %copy-done.13, f32[768,2304]{1,0:T(8,128)} %place.1.placed), custom_call_target="tpu_custom_call", output_to_operand_aliasing={{}: (3, {})} | custom-call | flops 1000000000 | bytes 3000000 | tf_op jit(solution)/shard_map/place_far/pallas_call | solution.py:366
  (70 shorter events, 9.9 us)
Async XLA Ops:
  3.7 15.8 %copy-start.15 = (s32[40,8]{0,1:T(8,128)S(1)}, s32[40,8]{0,1:T(8,128)}, u32[]{:S(2)}) copy-start(s32[40,8]{0,1:T(8,128)} %param.8) | copy-start | bytes 3844
  6.3 43.2 %collective-permute-start.1 = (bf16[2768,256]{1,0:T(8,128)(2,1)}, bf16[2768,256]{1,0:T(8,128)(2,1)S(1)}, u32[]{:S(2)}, u32[]{:S(2)}) collective-permute-start(bf16[2768,256]{1,0:T(8,128)(2,1)} %pad_maximum_fusion.1), channel_id=1, source_target_pairs={{1,0},{2,1},{3,2},{4,3},{5,4},{6,5},{7,6},{8,7},{9,8},{10,9},{11,1... | collective-permute-start | bytes 4251656 | tf_op jit(solution)/shard_map/ppermute | solution.py:385
  13.7 57.5 %collective-permute-start = (bf16[2768,256]{1,0:T(8,128)(2,1)}, bf16[2768,256]{1,0:T(8,128)(2,1)S(1)}, u32[]{:S(2)}, u32[]{:S(2)}) collective-permute-start(bf16[2768,256]{1,0:T(8,128)(2,1)} %pad_maximum_fusion.1), channel_id=1, source_target_pairs={{0,1},{1,2},{2,3},{3,4},{4,5},{5,6},{6,7},{7,8},{8,9},{9,10},{10,1... | collective-permute-start | bytes 4251656 | tf_op jit(solution)/shard_map/ppermute | solution.py:385
  15.7 32.5 %copy-start.9 = (bf16[208,256]{1,0:T(8,128)(2,1)}, bf16[208,256]{1,0:T(8,128)(2,1)S(1)}, u32[]{:S(2)}) copy-start(bf16[208,256]{1,0:T(8,128)(2,1)S(1)} %pad_maximum_fusion.3.q1) | copy-start | bytes 319492
  15.7 33.8 %collective-permute-start.2 = (bf16[208,256]{1,0:T(8,128)(2,1)S(1)}, bf16[208,256]{1,0:T(8,128)(2,1)S(1)}, u32[]{:S(2)}, u32[]{:S(2)}) collective-permute-start(bf16[208,256]{1,0:T(8,128)(2,1)S(1)} %pad_maximum_fusion.3.q1), channel_id=1, source_target_pairs={{2,0},{3,1},{4,2},{5,3},{6,4},{7,5},{8,6},{9,7},{10,8},{11,9},{12,... | collective-permute-start | bytes 319496 | tf_op jit(solution)/shard_map/ppermute | solution.py:385
  49.5 40.2 %copy-start.14 = (bf16[208,256]{1,0:T(8,128)(2,1)}, bf16[208,256]{1,0:T(8,128)(2,1)S(1)}, u32[]{:S(2)}) copy-start(bf16[208,256]{1,0:T(8,128)(2,1)S(1)} %collective-permute-done.2.q3) | copy-start | bytes 319492
  49.5 1.2 copy-start
  65.5 26.5 %collective-permute-start.3 = (bf16[640,640]{1,0:T(8,128)(2,1)}, bf16[640,640]{1,0:T(8,128)(2,1)S(1)}, u32[]{:S(2)}, u32[]{:S(2)}) collective-permute-start(bf16[640,640]{1,0:T(8,128)(2,1)} %get-tuple-element.35.outer3), channel_id=1, source_target_pairs={{0,1},{1,2},{2,3},{3,4},{4,5},{5,6},{6,7},{7,8},{8,9},{9,10},{10,1... | collective-permute-start | bytes 2457608 | tf_op jit(solution)/shard_map/ppermute | solution.py:385
  71.2 1.1 copy-start.1
  87.0 30.8 %collective-permute-start.4 = (bf16[640,640]{1,0:T(8,128)(2,1)}, bf16[640,640]{1,0:T(8,128)(2,1)S(1)}, u32[]{:S(2)}, u32[]{:S(2)}) collective-permute-start(bf16[640,640]{1,0:T(8,128)(2,1)} %get-tuple-element.40.outer0), channel_id=1, source_target_pairs={{0,1},{1,2},{2,3},{3,4},{4,5},{5,6},{6,7},{7,8},{8,9},{9,10},{10,1... | collective-permute-start | bytes 2457608 | tf_op jit(solution)/shard_map/ppermute | solution.py:385
  91.9 12.0 %copy-start.10 = (bf16[640,640]{1,0:T(8,128)(2,1)}, bf16[640,640]{1,0:T(8,128)(2,1)S(1)}, u32[]{:S(2)}) copy-start(bf16[640,640]{1,0:T(8,128)(2,1)S(1)} %collective-permute-done.3.got_h) | copy-start | bytes 2457604
  104.0 44.3 %collective-permute-start.5 = (bf16[1280,640]{1,0:T(8,128)(2,1)}, bf16[1280,640]{1,0:T(8,128)(2,1)S(1)}, u32[]{:S(2)}, u32[]{:S(2)}) collective-permute-start(bf16[1280,640]{1,0:T(8,128)(2,1)} %own_product1.1.inner), channel_id=1, source_target_pairs={{0,1},{1,2},{2,3},{3,4},{4,5},{5,6},{6,7},{7,8},{8,9},{9,10},{10,1... | collective-permute-start | bytes 4915208 | tf_op jit(solution)/shard_map/ppermute | solution.py:385
  117.8 11.8 %copy-start.11 = (bf16[640,640]{1,0:T(8,128)(2,1)}, bf16[640,640]{1,0:T(8,128)(2,1)S(1)}, u32[]{:S(2)}) copy-start(bf16[640,640]{1,0:T(8,128)(2,1)S(1)} %collective-permute-done.4.got_l) | copy-start | bytes 2457604
  129.6 13.3 %collective-permute-start.7 = (bf16[768,768]{1,0:T(8,128)(2,1)}, bf16[768,768]{1,0:T(8,128)(2,1)S(1)}, u32[]{:S(2)}, u32[]{:S(2)}) collective-permute-start(bf16[768,768]{1,0:T(8,128)(2,1)} %get-tuple-element.51), channel_id=1, source_target_pairs={{15,27},{31,45},{47,59},{63,77},{79,91},{95,109},{111,123}} | collective-permute-start | bytes 3538952 | tf_op jit(solution)/shard_map/ppermute | solution.py:439
  130.4 17.9 %collective-permute-start.6 = (bf16[768,768]{1,0:T(8,128)(2,1)}, bf16[768,768]{1,0:T(8,128)(2,1)S(1)}, u32[]{:S(2)}, u32[]{:S(2)}) collective-permute-start(bf16[768,768]{1,0:T(8,128)(2,1)} %get-tuple-element.52), channel_id=1, source_target_pairs={{15,31},{31,47},{47,63},{63,79},{79,95},{95,111},{111,127}} | collective-permute-start | bytes 3538952 | tf_op jit(solution)/shard_map/ppermute | solution.py:440
  131.1 11.8 %copy-start.7 = (bf16[768,768]{1,0:T(8,128)(2,1)S(1)}, bf16[768,768]{1,0:T(8,128)(2,1)}, u32[]{:S(2)}) copy-start(bf16[768,768]{1,0:T(8,128)(2,1)} %get-tuple-element.52) | copy-start | bytes 3538948
  142.9 5.4 %copy-start.6 = (bf16[768,768]{1,0:T(8,128)(2,1)S(1)}, bf16[768,768]{1,0:T(8,128)(2,1)}, u32[]{:S(2)}) copy-start(bf16[768,768]{1,0:T(8,128)(2,1)} %get-tuple-element.51) | copy-start | bytes 3538948
  142.9 5.4 %copy-start.8 = (bf16[768,768]{1,0:T(8,128)(2,1)S(1)}, bf16[768,768]{1,0:T(8,128)(2,1)}, u32[]{:S(2)}) copy-start(bf16[768,768]{1,0:T(8,128)(2,1)} %get-tuple-element.50) | copy-start | bytes 3538948
  148.3 1.2 copy-start.5
  201.6 10.5 %copy-start.2 = (bf16[4,48,2304]{2,1,0:T(8,128)(2,1)}, bf16[4,48,2304]{2,1,0:T(8,128)(2,1)S(1)}, u32[]{:S(2)}) copy-start(bf16[4,48,2304]{2,1,0:T(8,128)(2,1)S(1)} %all_to_all.18) | copy-start | bytes 2654212
  201.6 19.7 %collective-permute-start.8 = (bf16[192,2304]{1,0:T(8,128)(2,1)S(1)}, bf16[192,2304]{1,0:T(8,128)(2,1)S(1)}, u32[]{:S(2)}, u32[]{:S(2)}) collective-permute-start(bf16[192,2304]{1,0:T(8,128)(2,1)S(1)} %bitcast.24), channel_id=1, source_target_pairs={{0,4},{4,8},{8,12},{12,0},{1,5},{5,9},{9,13},{13,1},{2,6},{6,10},{... | collective-permute-start | bytes 2654216 | tf_op jit(solution)/shard_map/ppermute | solution.py:462
  202.1 19.3 %collective-permute-start.9 = (bf16[192,2304]{1,0:T(8,128)(2,1)S(1)}, bf16[192,2304]{1,0:T(8,128)(2,1)S(1)}, u32[]{:S(2)}, u32[]{:S(2)}) collective-permute-start(bf16[192,2304]{1,0:T(8,128)(2,1)S(1)} %bitcast.25), channel_id=1, source_target_pairs={{0,12},{4,0},{8,4},{12,8},{1,13},{5,1},{9,5},{13,9},{2,14},{6,2},{... | collective-permute-start | bytes 2654216 | tf_op jit(solution)/shard_map/ppermute | solution.py:463
  221.3 3.6 %copy-start.3 = (bf16[192,2304]{1,0:T(8,128)(2,1)}, bf16[192,2304]{1,0:T(8,128)(2,1)S(1)}, u32[]{:S(2)}) copy-start(bf16[192,2304]{1,0:T(8,128)(2,1)S(1)} %collective-permute-done.8.below) | copy-start | bytes 2654212
  221.5 3.4 %copy-start.4 = (bf16[192,2304]{1,0:T(8,128)(2,1)}, bf16[192,2304]{1,0:T(8,128)(2,1)S(1)}, u32[]{:S(2)}) copy-start(bf16[192,2304]{1,0:T(8,128)(2,1)S(1)} %collective-permute-done.9.above) | copy-start | bytes 2654212
  221.5 9.6 %collective-permute-start.10 = (bf16[96,2304]{1,0:T(8,128)(2,1)S(1)}, bf16[96,2304]{1,0:T(8,128)(2,1)S(1)}, u32[]{:S(2)}, u32[]{:S(2)}) collective-permute-start(bf16[96,2304]{1,0:T(8,128)(2,1)S(1)} %slice.42), channel_id=1, source_target_pairs={{0,4},{4,8},{8,12},{12,0},{1,5},{5,9},{9,13},{13,1},{2,6},{6,10},{... | collective-permute-start | bytes 1327112 | tf_op jit(solution)/shard_map/ppermute | solution.py:466
  222.0 9.1 %collective-permute-start.11 = (bf16[96,2304]{1,0:T(8,128)(2,1)S(1)}, bf16[96,2304]{1,0:T(8,128)(2,1)S(1)}, u32[]{:S(2)}, u32[]{:S(2)}) collective-permute-start(bf16[96,2304]{1,0:T(8,128)(2,1)S(1)} %slice.43), channel_id=1, source_target_pairs={{0,12},{4,0},{8,4},{12,8},{1,13},{5,1},{9,5},{13,9},{2,14},{6,2},{... | collective-permute-start | bytes 1327112 | tf_op jit(solution)/shard_map/ppermute | solution.py:467
  231.1 0.8 copy-start.12
  231.8 0.8 copy-start.13

commit v3 on v2

--- a/solution.py
+++ b/solution.py
@@ -90,7 +90,7 @@
                     acc[pcol[KP * i + m] // 2, rr, :] += z[:, m * 128 : m * 128 + 128]
             return c
 
-        lax.fori_loop(0, some, row, 0, unroll=2)
+        lax.fori_loop(0, some, row, 0, unroll=5)
 
     base = step * height
 
@@ -197,16 +197,22 @@
     )(wcol, p, pat)
 
 
-def own_kernel(which, wcol, p_ref, pat_hbm, rest0, rest2, out_ref, pt, pat, sem):
+def own_kernel(which, wcol, p_ref, pat_hbm, rest0, rest2, out_ref, pt, pat, rest, sems):
     mine = pat_hbm.at[pl.ds(FR, FR), pl.ds(which * BAND, BAND)]
-    copy = pltpu.make_async_copy(mine, pat, sem)
-    copy.start()
+    copies = [
+        pltpu.make_async_copy(mine, pat, sems.at[0]),
+        pltpu.make_async_copy(rest0, rest.at[0], sems.at[1]),
+        pltpu.make_async_copy(rest2, rest.at[1], sems.at[2]),
+    ]
+    for copy in copies:
+        copy.start()
     build_pt(wcol, p_ref, pt)
-    copy.wait()
-    for rest, start in ((rest0, 0), (rest2, BAND)):
+    for copy in copies:
+        copy.wait()
+    for n in range(2):
         def body(r):
-            here = shifted(r, start)
-            z = rest[r, :] + jnp.dot(pt[here, :], pat[...], preferred_element_type=F32)
+            here = shifted(r, n * BAND)
+            z = rest[n, r, :] + jnp.dot(pt[here, :], pat[...], preferred_element_type=F32)
             out_ref[here, :] = z.astype(BF)
 
         tiles(BAND, body)
@@ -216,12 +222,13 @@
     return pl.pallas_call(
         functools.partial(own_kernel, which),
         out_shape=jax.ShapeDtypeStruct((2 * BAND, BAND), BF),
-        in_specs=[SMEM, VMEM, ANY, VMEM, VMEM],
+        in_specs=[SMEM, VMEM, ANY, ANY, ANY],
         out_specs=VMEM,
         scratch_shapes=[
             pltpu.VMEM((2 * BAND, FR), BF),
             pltpu.VMEM((FR, BAND), BF),
-            pltpu.SemaphoreType.DMA,
+            pltpu.VMEM((2, BAND, BAND), F32),
+            pltpu.SemaphoreType.DMA((3,)),
         ],
         compiler_params=kernel_params(),
         cost_estimate=cost(1, 1),
@@ -230,15 +237,18 @@
 
 
 def level3_kernel(mine, flags, agg0, agg1, agg2, agg3, q0, q1, q2, q3, outer0, inner, outer3, *refs):
-    outs, (qt, u, q, sems) = refs[:2], refs[2:]
+    outs, (qt, u, q, rows, sems) = refs[:2], refs[2:]
     copies = []
     for s, ref in enumerate((q0, q1, q2, q3)):
         start = ref.shape[0] - Q_ROWS - NUM_ROWS
         copies.append(pltpu.make_async_copy(ref.at[pl.ds(start, Q_ROWS), :], q.at[s], sems.at[s]))
-        copies[-1].start()
+    for s, ref, start, count in ((4, inner, 1, 2), (5, outer0, 0, 1), (6, outer3, 3, 1)):
+        here = rows.at[pl.ds(start * BAND, count * BAND), :]
+        copies.append(pltpu.make_async_copy(ref, here, sems.at[s]))
+    for copy in copies:
+        copy.start()
     half = half_of((B, 2 * B))
     qt[...] = jnp.zeros_like(qt)
-    u[...] = jnp.zeros_like(u)
     for s, agg in enumerate((agg0, agg1, agg2, agg3)):
         copies[s].wait()
         for cp in range(CR // 2):
@@ -247,22 +257,22 @@
                 r = rows64(agg[AGG_AT + 2 * cp + e])
                 lanes = slice(cp * 128, cp * 128 + 128)
                 qt[s, r, lanes] = jnp.where(half == e, x, qt[s, r, lanes])
-    def expand(s, here):
-        u[flags[s]] += jnp.dot(qt[s], here, preferred_element_type=F32)
-
-    def middle(s, c):
-        expand(s + 1, inner[rows_at(s * BAND, BAND), :])
-        return c
-
-    expand(0, outer0[...])
-    lax.fori_loop(0, 2, middle, 0)
-    expand(3, outer3[...])
+
+    @pl.when(flags[4] == 1)
+    def none_yet():
+        u[1] = jnp.zeros((L3, BAND), F32)
+
+    for copy in copies[4:]:
+        copy.wait()
+    u[0] = jnp.dot(qt[1], rows[BAND : 2 * BAND, :], preferred_element_type=F32)
+    for s in (2, 0, 3):
+        u[flags[s]] += jnp.dot(qt[s], rows[s * BAND : s * BAND + BAND, :], preferred_element_type=F32)
 
     def finish(to):
         z = lax.dot_general(
-            u[to].astype(BF), qt[mine], (((1,), (1,)), ((), ())), preferred_element_type=F32
+            qt[mine], u[to].astype(BF), (((1,), (1,)), ((), ())), preferred_element_type=F32
         )
-        outs[to][...] = z.T.astype(BF)
+        outs[to][...] = z.astype(BF)
 
     finish(0)
     pl.when(flags[4] == 1)(lambda: finish(1))
@@ -276,13 +286,14 @@
     return pl.pallas_call(
         functools.partial(level3_kernel, mine),
         out_shape=[jax.ShapeDtypeStruct((L3, L3), BF)] * 2,
-        in_specs=[SMEM] * 5 + [ANY] * 4 + [VMEM] * 3,
+        in_specs=[SMEM] * 5 + [ANY] * 7,
         out_specs=[VMEM] * 2,
         scratch_shapes=[
             pltpu.VMEM((4, L3, BAND), BF),
             pltpu.VMEM((2, L3, BAND), F32),
             pltpu.VMEM((4, Q_ROWS, KP * B), BF),
-            pltpu.SemaphoreType.DMA((4,)),
+            pltpu.VMEM((4 * BAND, BAND), BF),
+            pltpu.SemaphoreType.DMA((7,)),
         ],
         compiler_params=kernel_params(),
         cost_estimate=cost(1, 1),
@@ -409,28 +420,24 @@
         return array[array.shape[0] - NUM_ROWS].astype(jnp.int32)
 
     pat = pta(cols, a_count, numbers, a_blocks, p_blocks)
-    far = moved(tail, -2)
-    pat, far = lax.optimization_barrier((pat, far))
-    nlow, nhigh, nfar = numbers_of(lower), numbers_of(higher), numbers_of(far)
-    aggs = (nlow, numbers, nhigh, nfar)
+    nlow, nhigh = numbers_of(lower), numbers_of(higher)
 
     low_h, up_h, rest2_low, rest2_up = halo_product(2, nhigh, higher, pat)
     got_h = moved(up_h, 1)
+    far, up_h = lax.optimization_barrier((higher[FR:], up_h))
+    far = moved(far, -1)
     low_l, up_l, rest0_low, rest0_up = halo_product(0, nlow, lower, pat)
     got_l = moved(up_l, 1)
     rest0_up, got_h = lax.optimization_barrier((rest0_up, got_h))
     up_m = own_product(1, numbers, p_blocks, pat, rest0_up, rest2_up)
     got_m = moved(up_m, 1)
-    rest0_low, up_m = lax.optimization_barrier((rest0_low, up_m))
-    low_m = own_product(0, numbers, p_blocks, pat, rest0_low, rest2_low)
-    low_m, got_l = lax.optimization_barrier((low_m, got_l))
+    nfar, got_l, up_m = lax.optimization_barrier((numbers_of(far), got_l, up_m))
+    aggs = (nlow, numbers, nhigh, nfar)
 
     qs = (lower, tail, higher, far)
     first, last = row == 0, row == row_size - 1
     ahead = row + 2 >= row_size
     flags = jnp.stack([first, row < 0, last, ahead, first | ahead]).astype(jnp.int32)
-    nfar, low_m = lax.optimization_barrier((nfar, low_m))
-    aggs = (nlow, numbers, nhigh, nfar)
     upper_c, upper_s = level3_parts(2, flags, aggs, qs, (up_l, up_m, up_h))
 
     def over(to):
@@ -438,7 +445,8 @@
 
     late_s = lax.ppermute(upper_c, ALL, over(lambda g: RELAYS[0] if g % 2 else RELAYS[1]))
     late_c = lax.ppermute(upper_s, ALL, over(lambda g: row_size - 1))
-    low_l, upper_c = lax.optimization_barrier((low_l, upper_c))
+    rest0_low, upper_c = lax.optimization_barrier((rest0_low, upper_c))
+    low_m = own_product(0, numbers, p_blocks, pat, rest0_low, rest2_low)
     lower_c, lower_s = level3_parts(1, flags, aggs, qs, (low_l, low_m, low_h))
     lower_c, got_m = lax.optimization_barrier((lower_c, got_m))
 

time: 238 us -> 236 us (level)
  Pallas kernels: 118 us -> 114 us
  transfers between devices with their start and end apart: 12 -> 12, of which waited for: 6 -> 4; matrix products, arithmetic and copies ran while one was open for 3% -> 3% of each run, Pallas kernels for 49% -> 47%
where the time goes in v3:
time: 236 us; the launch traced here: 235 us
  Pallas kernels  114 us (48%)
  blocking collectives  52.3 us (22%)
  starting transfers between devices  31.1 us (13%)
  waiting for transfers between devices  19.6 us (8%)
  other arithmetic  11.1 us (5%)
  local copies, waits for them, and re-layouts  6.22 us (3%)
    all_to_all x1, blocking collectives, per_device(): lax.all_to_all(main, ROW, 0, 0, tiled=True).reshape(row_size, chunk, 2 * L3)  37.2 us
    pallas_call x2, Pallas kernels, halo_product(): pl.pallas_call(functools.partial(halo_kernel, part), out_shape=[jax.Shape...  29.5 us
    pallas_call x1, Pallas kernels, pta(): pl.pallas_call(pta_kernel, grid=(steps,), out_shape=jax.ShapeDtypeStruct(...  25.3 us
    ppermute x6, starting transfers between devices, moved(): return lax.ppermute(array, ALL, pairs)  23 us
    pallas_call x2, Pallas kernels, own_product(): pl.pallas_call(functools.partial(own_kernel, which), out_shape=jax.ShapeD...  22.7 us
    pallas_call x2, Pallas kernels, level3_parts(): pl.pallas_call(functools.partial(level3_kernel, mine), out_shape=[jax.Sha...  22 us
    all_to_all x1, blocking collectives, per_device(): whole = lax.all_to_all(jnp.tile(whole, (sx, 1)), 'x', 0, 0, tiled=True)  15.1 us
    ppermute x1, waiting for transfers between devices, per_device(): below = lax.ppermute(whole, 'z', onward)  10.3 us
  transfers between devices with their start and end apart: 12, of which 4 were waited for; matrix products, arithmetic and copies ran while one was open for 3% of the time, Pallas kernels for 47%

profile of v3, /device:TPU:8, one launch (start us, length us, event | category | flops | bytes accessed | tf_op | source)
XLA Modules:
  0.0 234.8 jit_solution(12338686150676042992)
XLA Ops:
  2.4 1.1 reshape.112
  3.7 2.5 %pad_maximum_fusion.1 = bf16[2768,256]{1,0:T(8,128)(2,1)} fusion(bf16[16,256]{1,0:T(8,128)(2,1)S(1)} %pad.9, bf16[192,256]{1,0:T(8,128)(2,1)S(1)} %bitcast.27, bf16[2560,256]{1,0:T(8,128)(2,1)} %p_ref.5), kind=kLoop, calls=%fused_computation.3 | loop fusion | flops 4251648 | bytes 2834432 | tf_op jit(solution)/shard_map/concatenate | solution.py:415
  6.3 7.5 %collective-permute-start.1 = (bf16[2768,256]{1,0:T(8,128)(2,1)}, bf16[2768,256]{1,0:T(8,128)(2,1)S(1)}, u32[]{:S(2)}, u32[]{:S(2)}) collective-permute-start(bf16[2768,256]{1,0:T(8,128)(2,1)} %pad_maximum_fusion.1), channel_id=1, source_target_pairs={{1,0},{2,1},{3,2},{4,3},{5,4},{6,5},{7,6},{8,7},{9,8},{10,9},{11,1... | collective-permute-start | bytes 4251656 | tf_op jit(solution)/shard_map/ppermute | solution.py:396
  13.7 1.9 collective-permute-start
  17.2 25.3 %pta.1.pat_hbm = bf16[7680,1280]{1,0:T(8,128)(2,1)} custom-call(s32[40,8]{1,0:T(8,128)} %broadcast_subtract_fusion.cols, s32[40]{0:T(128)} %count.1, s32[256]{0:T(256)} %pad_add_fusion.pcol.wcol.agg1, bf16[2560,512]{1,0:T(8,128)(2,1)} %a_ref.1, bf16[2560,256]{1,0:T(8,128)(2,1)} %p_ref.5), custom_call_target="tpu_custom_call" | custom-call | flops 12000000000 | bytes 24000000 | tf_op jit(solution)/shard_map/pta/pallas_call | solution.py:110
  42.5 2.9 %collective-permute-done.1.p_hbm.q2 = bf16[2768,256]{1,0:T(8,128)(2,1)S(1)} collective-permute-done((bf16[2768,256]{1,0:T(8,128)(2,1)}, bf16[2768,256]{1,0:T(8,128)(2,1)S(1)}, u32[]{:S(2)}, u32[]{:S(2)}) %collective-permute-start.1) | collective-permute-done | bytes 1417248 | tf_op jit(solution)/shard_map/ppermute | solution.py:396
  46.5 14.8 %halo_product2.1 = (bf16[640,640]{1,0:T(8,128)(2,1)}, bf16[640,640]{1,0:T(8,128)(2,1)}, f32[640,640]{1,0:T(8,128)}, f32[640,640]{1,0:T(8,128)}) custom-call(s32[256]{0:T(256)} %bitcast.32, bf16[2768,256]{1,0:T(8,128)(2,1)} %copy-done, bf16[7680,1280]{1,0:T(8,128)(2,1)} %pta.1.pat_hbm), custom_call_target="tpu_custom_call" | custom-call | flops 8000000000 | bytes 14000000 | tf_op jit(solution)/shard_map/halo_product2/pallas_call | solution.py:183
  61.3 1.9 collective-permute-start.4
  64.4 14.8 %halo_product0.1 = (bf16[640,640]{1,0:T(8,128)(2,1)}, bf16[640,640]{1,0:T(8,128)(2,1)}, f32[640,640]{1,0:T(8,128)}, f32[640,640]{1,0:T(8,128)}) custom-call(s32[256]{0:T(256)} %bitcast.35, bf16[2768,256]{1,0:T(8,128)(2,1)} %copy-done.1, bf16[7680,1280]{1,0:T(8,128)(2,1)} %pta.1.pat_hbm), custom_call_target="tpu_custom_call" | custom-call | flops 8000000000 | bytes 14000000 | tf_op jit(solution)/shard_map/halo_product0/pallas_call | solution.py:183
  79.1 1.9 collective-permute-start.3
  81.1 0.9 slice.50
  82.0 7.9 %collective-permute-start.2 = (bf16[208,256]{1,0:T(8,128)(2,1)S(1)}, bf16[208,256]{1,0:T(8,128)(2,1)S(1)}, u32[]{:S(2)}, u32[]{:S(2)}) collective-permute-start(bf16[208,256]{1,0:T(8,128)(2,1)S(1)} %slice.50), channel_id=1, source_target_pairs={{1,0},{2,1},{3,2},{4,3},{5,4},{6,5},{7,6},{8,7},{9,8},{10,9},{11,1... | collective-permute-start | bytes 319496 | tf_op jit(solution)/shard_map/ppermute | solution.py:396
  91.1 11.5 %own_product1.1.inner = bf16[1280,640]{1,0:T(8,128)(2,1)} custom-call(s32[256]{0:T(256)} %pad_add_fusion.pcol.wcol.agg1, bf16[2560,256]{1,0:T(8,128)(2,1)} %p_ref.5, bf16[7680,1280]{1,0:T(8,128)(2,1)} %pta.1.pat_hbm, f32[640,640]{1,0:T(8,128)} %get-tuple-element.32.rest0, f32[640,640]{1,0:T(8,128)} %get-tuple-element.33.rest2), custom_call_target="tpu_custom_call" | custom-call | flops 1000000000 | bytes 1000000 | tf_op jit(solution)/shard_map/own_product1/pallas_call | solution.py:222
  102.7 1.9 collective-permute-start.5
  105.2 10.8 %level3_parts2.1 = (bf16[768,768]{1,0:T(8,128)(2,1)}, bf16[768,768]{1,0:T(8,128)(2,1)}) custom-call(s32[5]{0:T(128)} %convert_element_type.93.flags, s32[256]{0:T(256)} %bitcast.36, s32[256]{0:T(256)} %pad_add_fusion.pcol.wcol.agg1, s32[256]{0:T(256)} %bitcast.33, s32[256]{0:T(256)} %bitcast.38, bf16[2768,256]{1,0:T(8,128)(2,1)} %copy-done.1, ...), custom_call_target="tpu_custom_call" | custom-call | flops 1000000000 | bytes 1000000 | tf_op jit(solution)/shard_map/level3_parts2/pallas_call | solution.py:286
  116.1 0.7 collective-permute-start.7
  116.8 0.7 collective-permute-start.6
  117.6 11.2 %own_product0.1.inner.low_m = bf16[1280,640]{1,0:T(8,128)(2,1)} custom-call(s32[256]{0:T(256)} %pad_add_fusion.pcol.wcol.agg1, bf16[2560,256]{1,0:T(8,128)(2,1)} %p_ref.5, bf16[7680,1280]{1,0:T(8,128)(2,1)} %pta.1.pat_hbm, f32[640,640]{1,0:T(8,128)} %get-tuple-element.40.rest0, f32[640,640]{1,0:T(8,128)} %get-tuple-element.41.rest2), custom_call_target="tpu_custom_call" | custom-call | flops 1000000000 | bytes 1000000 | tf_op jit(solution)/shard_map/own_product0/pallas_call | solution.py:222
  128.8 11.2 %level3_parts1.1 = (bf16[768,768]{1,0:T(8,128)(2,1)}, bf16[768,768]{1,0:T(8,128)(2,1)}) custom-call(s32[5]{0:T(128)} %convert_element_type.93.flags, s32[256]{0:T(256)} %bitcast.37, s32[256]{0:T(256)} %pad_add_fusion.pcol.wcol.agg1, s32[256]{0:T(256)} %bitcast.34, s32[256]{0:T(256)} %bitcast.39, bf16[2768,256]{1,0:T(8,128)(2,1)} %copy-done.1, ...), custom_call_target="tpu_custom_call" | custom-call | flops 1000000000 | bytes 1000000 | tf_op jit(solution)/shard_map/level3_parts1/pallas_call | solution.py:286
  140.0 1.9 add_convert_fusion
  141.9 3.8 %collective-permute-done.5.got_m = bf16[1280,640]{1,0:T(8,128)(2,1)S(1)} collective-permute-done((bf16[1280,640]{1,0:T(8,128)(2,1)}, bf16[1280,640]{1,0:T(8,128)(2,1)S(1)}, u32[]{:S(2)}, u32[]{:S(2)}) %collective-permute-start.5) | collective-permute-done | bytes 1638432 | tf_op jit(solution)/shard_map/ppermute | solution.py:396
  147.1 37.2 %all_to_all.17 = bf16[16,48,1536]{2,1,0:T(8,128)(2,1)S(1)} all-to-all(bf16[16,48,1536]{2,1,0:T(8,128)(2,1)S(1)} %bitcast.23), channel_id=1, replica_groups=mesh['grp'=8,'z'=4,'x'=4] {'z','x'}, dimensions={0} | all-to-all | bytes 4718592 | tf_op jit(solution)/shard_map/all_to_all | solution.py:460
  184.6 15.1 %all_to_all.18 = bf16[4,48,2304]{2,1,0:T(8,128)(2,1)S(1)} all-to-all(bf16[4,48,2304]{2,1,0:T(8,128)(2,1)S(1)} %tile.2), channel_id=1, replica_groups=mesh['grp'=8,'z'=4,'x'=4] {'x'}, dimensions={0} | all-to-all | bytes 1769472 | tf_op jit(solution)/shard_map/all_to_all | solution.py:466
  199.7 3.2 %collective-permute-start.9 = (bf16[192,2304]{1,0:T(8,128)(2,1)S(1)}, bf16[192,2304]{1,0:T(8,128)(2,1)S(1)}, u32[]{:S(2)}, u32[]{:S(2)}) collective-permute-start(bf16[192,2304]{1,0:T(8,128)(2,1)S(1)} %bitcast.25), channel_id=1, source_target_pairs={{0,12},{4,0},{8,4},{12,8},{1,13},{5,1},{9,5},{13,9},{2,14},{6,2},{... | collective-permute-start | bytes 2654216 | tf_op jit(solution)/shard_map/ppermute | solution.py:471
  202.9 7.2 %level2_rows.1 = bf16[640,3200]{1,0:T(8,128)(2,1)} custom-call(bf16[640,640]{1,0:T(8,128)(2,1)} %get-tuple-element.35.outer0.low_l, bf16[1280,640]{1,0:T(8,128)(2,1)} %own_product0.1.inner.low_m, bf16[640,640]{1,0:T(8,128)(2,1)} %get-tuple-element.42.outer3.low_h, bf16[640,640]{1,0:T(8,128)(2,1)} %copy-done.10, bf16[1280,640]{1,0:T(8,128)(2,1)} %copy-done.5, ...), custom_call_target="tpu_custom_call" | custom-call | flops 1000000000 | bytes 14000000 | tf_op jit(solution)/shard_map/level2_rows/pallas_call | solution.py:317
  210.1 10.3 %collective-permute-done.8.below = bf16[192,2304]{1,0:T(8,128)(2,1)S(1)} collective-permute-done((bf16[192,2304]{1,0:T(8,128)(2,1)S(1)}, bf16[192,2304]{1,0:T(8,128)(2,1)S(1)}, u32[]{:S(2)}, u32[]{:S(2)}) %collective-permute-start.8) | collective-permute-done | bytes 884768 | tf_op jit(solution)/shard_map/ppermute | solution.py:470
  220.6 3.3 %collective-permute-start.11 = (bf16[96,2304]{1,0:T(8,128)(2,1)S(1)}, bf16[96,2304]{1,0:T(8,128)(2,1)S(1)}, u32[]{:S(2)}, u32[]{:S(2)}) collective-permute-start(bf16[96,2304]{1,0:T(8,128)(2,1)S(1)} %slice.47), channel_id=1, source_target_pairs={{0,12},{4,0},{8,4},{12,8},{1,13},{5,1},{9,5},{13,9},{2,14},{6,2},{... | collective-permute-start | bytes 1327112 | tf_op jit(solution)/shard_map/ppermute | solution.py:475
  223.8 4.4 %place.1.placed = f32[768,2304]{1,0:T(8,128)} custom-call(s32[1]{0:T(128)} %bitcast.18.z, bf16[192,2304]{1,0:T(8,128)(2,1)} %bitcast.26, bf16[192,2304]{1,0:T(8,128)(2,1)} %copy-done.3, bf16[192,2304]{1,0:T(8,128)(2,1)} %copy-done.4), custom_call_target="tpu_custom_call" | custom-call | flops 1000000000 | bytes 8000000 | tf_op jit(solution)/shard_map/place/pallas_call | solution.py:360
  228.2 2.6 %collective-permute-done.10.half_a = bf16[96,2304]{1,0:T(8,128)(2,1)S(1)} collective-permute-done((bf16[96,2304]{1,0:T(8,128)(2,1)S(1)}, bf16[96,2304]{1,0:T(8,128)(2,1)S(1)}, u32[]{:S(2)}, u32[]{:S(2)}) %collective-permute-start.10) | collective-permute-done | bytes 442400 | tf_op jit(solution)/shard_map/ppermute | solution.py:474
  230.8 0.8 copy-done.11
  231.6 0.8 copy-done.12
  232.3 2.5 %place_far.1 = f32[768,2304]{1,0:T(8,128)} custom-call(s32[1]{0:T(128)} %bitcast.18.z, bf16[96,2304]{1,0:T(8,128)(2,1)} %copy-done.11, bf16[96,2304]{1,0:T(8,128)(2,1)} %copy-done.12, f32[768,2304]{1,0:T(8,128)} %place.1.placed), custom_call_target="tpu_custom_call", output_to_operand_aliasing={{}: (3, {})} | custom-call | flops 1000000000 | bytes 3000000 | tf_op jit(solution)/shard_map/place_far/pallas_call | solution.py:377
  (69 shorter events, 9.5 us)
Async XLA Ops:
  3.7 12.1 %copy-start.14 = (s32[40,8]{0,1:T(8,128)S(1)}, s32[40,8]{0,1:T(8,128)}, u32[]{:S(2)}) copy-start(s32[40,8]{0,1:T(8,128)} %param.8) | copy-start | bytes 3844
  6.3 39.1 %collective-permute-start.1 = (bf16[2768,256]{1,0:T(8,128)(2,1)}, bf16[2768,256]{1,0:T(8,128)(2,1)S(1)}, u32[]{:S(2)}, u32[]{:S(2)}) collective-permute-start(bf16[2768,256]{1,0:T(8,128)(2,1)} %pad_maximum_fusion.1), channel_id=1, source_target_pairs={{1,0},{2,1},{3,2},{4,3},{5,4},{6,5},{7,6},{8,7},{9,8},{10,9},{11,1... | collective-permute-start | bytes 4251656 | tf_op jit(solution)/shard_map/ppermute | solution.py:396
  13.7 49.5 %collective-permute-start = (bf16[2768,256]{1,0:T(8,128)(2,1)}, bf16[2768,256]{1,0:T(8,128)(2,1)S(1)}, u32[]{:S(2)}, u32[]{:S(2)}) collective-permute-start(bf16[2768,256]{1,0:T(8,128)(2,1)} %pad_maximum_fusion.1), channel_id=1, source_target_pairs={{0,1},{1,2},{2,3},{3,4},{4,5},{5,6},{6,7},{7,8},{8,9},{9,10},{10,1... | collective-permute-start | bytes 4251656 | tf_op jit(solution)/shard_map/ppermute | solution.py:396
  45.4 1.2 copy-start
  61.3 29.8 %collective-permute-start.4 = (bf16[640,640]{1,0:T(8,128)(2,1)}, bf16[640,640]{1,0:T(8,128)(2,1)S(1)}, u32[]{:S(2)}, u32[]{:S(2)}) collective-permute-start(bf16[640,640]{1,0:T(8,128)(2,1)} %get-tuple-element.38.outer3), channel_id=1, source_target_pairs={{0,1},{1,2},{2,3},{3,4},{4,5},{5,6},{6,7},{7,8},{8,9},{9,10},{10,1... | collective-permute-start | bytes 2457608 | tf_op jit(solution)/shard_map/ppermute | solution.py:396
  63.3 1.1 copy-start.1
  79.1 26.1 %collective-permute-start.3 = (bf16[640,640]{1,0:T(8,128)(2,1)}, bf16[640,640]{1,0:T(8,128)(2,1)S(1)}, u32[]{:S(2)}, u32[]{:S(2)}) collective-permute-start(bf16[640,640]{1,0:T(8,128)(2,1)} %get-tuple-element.30.outer0), channel_id=1, source_target_pairs={{0,1},{1,2},{2,3},{3,4},{4,5},{5,6},{6,7},{7,8},{8,9},{9,10},{10,1... | collective-permute-start | bytes 2457608 | tf_op jit(solution)/shard_map/ppermute | solution.py:396
  82.0 22.6 %collective-permute-start.2 = (bf16[208,256]{1,0:T(8,128)(2,1)S(1)}, bf16[208,256]{1,0:T(8,128)(2,1)S(1)}, u32[]{:S(2)}, u32[]{:S(2)}) collective-permute-start(bf16[208,256]{1,0:T(8,128)(2,1)S(1)} %slice.50), channel_id=1, source_target_pairs={{1,0},{2,1},{3,2},{4,3},{5,4},{6,5},{7,6},{8,7},{9,8},{10,9},{11,1... | collective-permute-start | bytes 319496 | tf_op jit(solution)/shard_map/ppermute | solution.py:396
  91.1 11.5 %copy-start.9 = (bf16[640,640]{1,0:T(8,128)(2,1)}, bf16[640,640]{1,0:T(8,128)(2,1)S(1)}, u32[]{:S(2)}) copy-start(bf16[640,640]{1,0:T(8,128)(2,1)S(1)} %collective-permute-done.4.got_h) | copy-start | bytes 2457604
  102.7 43.0 %collective-permute-start.5 = (bf16[1280,640]{1,0:T(8,128)(2,1)}, bf16[1280,640]{1,0:T(8,128)(2,1)S(1)}, u32[]{:S(2)}, u32[]{:S(2)}) collective-permute-start(bf16[1280,640]{1,0:T(8,128)(2,1)} %own_product1.1.inner), channel_id=1, source_target_pairs={{0,1},{1,2},{2,3},{3,4},{4,5},{5,6},{6,7},{7,8},{8,9},{9,10},{10,1... | collective-permute-start | bytes 4915208 | tf_op jit(solution)/shard_map/ppermute | solution.py:396
  104.6 0.6 copy-start.13
  105.2 10.8 %copy-start.10 = (bf16[640,640]{1,0:T(8,128)(2,1)}, bf16[640,640]{1,0:T(8,128)(2,1)S(1)}, u32[]{:S(2)}) copy-start(bf16[640,640]{1,0:T(8,128)(2,1)S(1)} %collective-permute-done.3.got_l) | copy-start | bytes 2457604
  116.1 23.9 %collective-permute-start.7 = (bf16[768,768]{1,0:T(8,128)(2,1)}, bf16[768,768]{1,0:T(8,128)(2,1)S(1)}, u32[]{:S(2)}, u32[]{:S(2)}) collective-permute-start(bf16[768,768]{1,0:T(8,128)(2,1)} %get-tuple-element.45), channel_id=1, source_target_pairs={{15,27},{31,45},{47,59},{63,77},{79,91},{95,109},{111,123}} | collective-permute-start | bytes 3538952 | tf_op jit(solution)/shard_map/ppermute | solution.py:446
  116.8 28.9 %collective-permute-start.6 = (bf16[768,768]{1,0:T(8,128)(2,1)}, bf16[768,768]{1,0:T(8,128)(2,1)S(1)}, u32[]{:S(2)}, u32[]{:S(2)}) collective-permute-start(bf16[768,768]{1,0:T(8,128)(2,1)} %get-tuple-element.46), channel_id=1, source_target_pairs={{15,31},{31,47},{47,63},{63,79},{79,95},{95,111},{111,127}} | collective-permute-start | bytes 3538952 | tf_op jit(solution)/shard_map/ppermute | solution.py:447
  128.8 11.2 %copy-start.7 = (bf16[768,768]{1,0:T(8,128)(2,1)S(1)}, bf16[768,768]{1,0:T(8,128)(2,1)}, u32[]{:S(2)}) copy-start(bf16[768,768]{1,0:T(8,128)(2,1)} %get-tuple-element.46) | copy-start | bytes 3538948
  140.0 5.7 %copy-start.6 = (bf16[768,768]{1,0:T(8,128)(2,1)S(1)}, bf16[768,768]{1,0:T(8,128)(2,1)}, u32[]{:S(2)}) copy-start(bf16[768,768]{1,0:T(8,128)(2,1)} %get-tuple-element.45) | copy-start | bytes 3538948
  140.0 5.7 %copy-start.8 = (bf16[768,768]{1,0:T(8,128)(2,1)S(1)}, bf16[768,768]{1,0:T(8,128)(2,1)}, u32[]{:S(2)}) copy-start(bf16[768,768]{1,0:T(8,128)(2,1)} %get-tuple-element.44) | copy-start | bytes 3538948
  145.7 1.2 copy-start.5
  199.7 10.5 %copy-start.2 = (bf16[4,48,2304]{2,1,0:T(8,128)(2,1)}, bf16[4,48,2304]{2,1,0:T(8,128)(2,1)S(1)}, u32[]{:S(2)}) copy-start(bf16[4,48,2304]{2,1,0:T(8,128)(2,1)S(1)} %all_to_all.18) | copy-start | bytes 2654212
  199.7 20.7 %collective-permute-start.8 = (bf16[192,2304]{1,0:T(8,128)(2,1)S(1)}, bf16[192,2304]{1,0:T(8,128)(2,1)S(1)}, u32[]{:S(2)}, u32[]{:S(2)}) collective-permute-start(bf16[192,2304]{1,0:T(8,128)(2,1)S(1)} %bitcast.24), channel_id=1, source_target_pairs={{0,4},{4,8},{8,12},{12,0},{1,5},{5,9},{9,13},{13,1},{2,6},{6,10},{... | collective-permute-start | bytes 2654216 | tf_op jit(solution)/shard_map/ppermute | solution.py:470
  199.7 20.7 %collective-permute-start.9 = (bf16[192,2304]{1,0:T(8,128)(2,1)S(1)}, bf16[192,2304]{1,0:T(8,128)(2,1)S(1)}, u32[]{:S(2)}, u32[]{:S(2)}) collective-permute-start(bf16[192,2304]{1,0:T(8,128)(2,1)S(1)} %bitcast.25), channel_id=1, source_target_pairs={{0,12},{4,0},{8,4},{12,8},{1,13},{5,1},{9,5},{13,9},{2,14},{6,2},{... | collective-permute-start | bytes 2654216 | tf_op jit(solution)/shard_map/ppermute | solution.py:471
  220.4 3.5 %copy-start.3 = (bf16[192,2304]{1,0:T(8,128)(2,1)}, bf16[192,2304]{1,0:T(8,128)(2,1)S(1)}, u32[]{:S(2)}) copy-start(bf16[192,2304]{1,0:T(8,128)(2,1)S(1)} %collective-permute-done.8.below) | copy-start | bytes 2654212
  220.4 3.4 %copy-start.4 = (bf16[192,2304]{1,0:T(8,128)(2,1)}, bf16[192,2304]{1,0:T(8,128)(2,1)S(1)}, u32[]{:S(2)}) copy-start(bf16[192,2304]{1,0:T(8,128)(2,1)S(1)} %collective-permute-done.9.above) | copy-start | bytes 2654212
  220.4 10.4 %collective-permute-start.10 = (bf16[96,2304]{1,0:T(8,128)(2,1)S(1)}, bf16[96,2304]{1,0:T(8,128)(2,1)S(1)}, u32[]{:S(2)}, u32[]{:S(2)}) collective-permute-start(bf16[96,2304]{1,0:T(8,128)(2,1)S(1)} %slice.46), channel_id=1, source_target_pairs={{0,4},{4,8},{8,12},{12,0},{1,5},{5,9},{9,13},{13,1},{2,6},{6,10},{... | collective-permute-start | bytes 1327112 | tf_op jit(solution)/shard_map/ppermute | solution.py:474
  220.6 10.3 %collective-permute-start.11 = (bf16[96,2304]{1,0:T(8,128)(2,1)S(1)}, bf16[96,2304]{1,0:T(8,128)(2,1)S(1)}, u32[]{:S(2)}, u32[]{:S(2)}) collective-permute-start(bf16[96,2304]{1,0:T(8,128)(2,1)S(1)} %slice.47), channel_id=1, source_target_pairs={{0,12},{4,0},{8,4},{12,8},{1,13},{5,1},{9,5},{13,9},{2,14},{6,2},{... | collective-permute-start | bytes 1327112 | tf_op jit(solution)/shard_map/ppermute | solution.py:475
  230.8 0.8 copy-start.11
  231.6 0.8 copy-start.12
